TPU v7x, 32 devices: a whole 2x2x4 slice. The times are simulated.
32 devices in a mesh: dp: 16 (over z, y, core), mp: 2 (over x).
Axes of the slice: x: 2, y: 2, z: 4, core: 2. Of those that a mesh axis runs over, the one named last changes fastest.
Arguments:
- inputs: bfloat16 [2, 4096, 2048], P(None, 'dp'), may hold values from -6 to 6
- seq_starts: int32 [2, 4096], P(None, 'dp'), may hold values from 0 to 4095, as said below
- cotangent: bfloat16 [2, 4096, 2048], P(None, 'dp'), may hold values from -6 to 6
- attn_gain: bfloat16 [2048], P('dp'), may hold values from 0.5 to 1.5
- query_weight: bfloat16 [2048, 2048], P('dp', 'mp'), may hold values from -0.125 to 0.125
- key_matrix: bfloat16 [2048, 512], P('dp', 'mp'), may hold values from -0.125 to 0.125
- value_matrix: bfloat16 [2048, 512], P('dp', 'mp'), may hold values from -0.125 to 0.125
- out_weight: bfloat16 [2048, 2048], P('mp', 'dp'), may hold values from -0.5 to 0.5
- mlp_gain: bfloat16 [2048], P('dp'), may hold values from 0.5 to 1.5
- gate_weight: bfloat16 [2048, 8192], P('dp', 'mp'), may hold values from -0.125 to 0.125
- up_weight: bfloat16 [2048, 8192], P('dp', 'mp'), may hold values from -0.125 to 0.125
- down_weight: bfloat16 [8192, 2048], P('mp', 'dp'), may hold values from -0.125 to 0.125
Outputs:
- output: bfloat16 [2, 4096, 2048], P(None, 'dp')
- input_grad: float32 [2, 4096, 2048], P(None, 'dp')
- grad_attn_gain: float32 [2048], P('dp')
- grad_query: float32 [2048, 2048], P('dp', 'mp')
- grad_key: float32 [2048, 512], P('dp', 'mp')
- grad_value: float32 [2048, 512], P('dp', 'mp')
- grad_out: float32 [2048, 2048], P('mp', 'dp')
- grad_mlp_gain: float32 [2048], P('dp')
- grad_gate: float32 [2048, 8192], P('dp', 'mp')
- grad_up: float32 [2048, 8192], P('dp', 'mp')
- grad_down: float32 [8192, 2048], P('mp', 'dp')
Inputs may be any that keep to these rules, and one draw needn't show every extreme that they name: `seq_starts`: each entry is the index, within its micro-batch of 4096 tokens, of the first token of its sequence: entries never fall along a micro-batch, never exceed their own index, every multiple of 256 begins a sequence, and the last token of a micro-batch begins a sequence of its own.
All inputs are finite; a program needn't handle non-finite values.
Results may differ from a plain program's by a relative error of at most 0.015.
Values may be sent and summed in bfloat16 or wider, within the bound.
No kernel may reach another device: no remote copies, remote signals or barrier semaphores. Data moves between devices by JAX's collectives and lax.ppermute only.
A program may use at most 320 MiB of HBM per device.

v0:
```python
import math

import jax
import jax.numpy as jnp
from jax import lax
from jax.sharding import PartitionSpec as P

HEAD_SIZE = 64


EPSILON = 1e-05


def rms_parts(values_in, gain):
    inverse = lax.rsqrt(jnp.mean(values_in * values_in, axis=-1, keepdims=True) + EPSILON)
    normed = values_in * inverse
    return (normed, inverse, normed * gain)


def rms_back(grad_scaled, normed, inverse, gain):
    grad_normed = grad_scaled * gain
    inner_mean = jnp.mean(grad_normed * normed, axis=-1, keepdims=True)
    return (inverse * (grad_normed - normed * inner_mean), jnp.sum(grad_scaled * normed, axis=0))


def rope_tables(positions, head_dim):
    halfway = head_dim // 2
    frequency = 500000.0 ** (-(jnp.arange(halfway, dtype=jnp.float32) * 2.0 / head_dim))
    angles = positions.astype(jnp.float32)[:, None] * frequency[None, :]
    angles = jnp.concatenate([angles, angles], axis=1)
    return (jnp.cos(angles), jnp.sin(angles))


def rotate_half(head_rows, cosine_lookup, sine_lookup, direction):
    halfway = head_rows.shape[-1] // 2
    turned = jnp.concatenate([-head_rows[..., halfway:], head_rows[..., :halfway]], axis=-1)
    return head_rows * cosine_lookup[:, None, :] + direction * turned * sine_lookup[:, None, :]


def per_device(
    inputs,
    seq_starts,
    cotangent,
    attn_gain,
    query_weight,
    key_matrix,
    value_matrix,
    out_weight,
    mlp_gain,
    gate_weight,
    up_weight,
    down_weight,
):
    micro_count, tok_rows, width = inputs.shape
    local_heads = query_weight.shape[1] // HEAD_SIZE
    local_groups = key_matrix.shape[1] // HEAD_SIZE
    group_width = local_heads // local_groups
    score_scale = 1.0 / math.sqrt(HEAD_SIZE)
    offset = lax.axis_index("dp") * tok_rows
    local_pos = jnp.arange(tok_rows, dtype=jnp.int32)

    def masked_scores(grouped_queries, key_rot, allowed):
        raw = (
            jnp.einsum(
                "qkgd,skd->kgqs", grouped_queries, key_rot, preferred_element_type=jnp.float32
            )
            * score_scale
        )
        return jnp.where(allowed[None, None], raw, -1e30)

    acc_attn_gain = jnp.zeros((width,), jnp.float32)
    acc_query = jnp.zeros((width, query_weight.shape[1]), jnp.float32)
    acc_key = jnp.zeros((width, key_matrix.shape[1]), jnp.float32)
    acc_value = jnp.zeros((width, value_matrix.shape[1]), jnp.float32)
    acc_out = jnp.zeros((out_weight.shape[0], width), jnp.float32)
    acc_mlp_gain = jnp.zeros((width,), jnp.float32)
    acc_gate = jnp.zeros((width, gate_weight.shape[1]), jnp.float32)
    acc_up = jnp.zeros((width, up_weight.shape[1]), jnp.float32)
    acc_down = jnp.zeros((down_weight.shape[0], width), jnp.float32)
    outputs = []
    input_grads = []
    for batch_index in range(micro_count):
        attn_set = (
            lax.all_gather(query_weight, "dp", axis=0, tiled=True),
            lax.all_gather(key_matrix, "dp", axis=0, tiled=True),
            lax.all_gather(value_matrix, "dp", axis=0, tiled=True),
            lax.all_gather(out_weight, "dp", axis=1, tiled=True),
            lax.all_gather(attn_gain, "dp", axis=0, tiled=True),
        )
        feed_set = (
            lax.all_gather(gate_weight, "dp", axis=0, tiled=True),
            lax.all_gather(up_weight, "dp", axis=0, tiled=True),
            lax.all_gather(down_weight, "dp", axis=1, tiled=True),
            lax.all_gather(mlp_gain, "dp", axis=0, tiled=True),
        )
        query_full, key_full, value_full, out_full, attn_gain_full = attn_set
        gate_full, up_full, down_full, mlp_gain_full = feed_set
        attn_scale = attn_gain_full.astype(jnp.float32)
        mlp_scale = mlp_gain_full.astype(jnp.float32)
        rows_in = inputs[batch_index].astype(jnp.float32)
        start_offsets = seq_starts[batch_index]
        positions = offset + local_pos - start_offsets
        cosine_lookup, sine_lookup = rope_tables(positions, HEAD_SIZE)
        allowed = (start_offsets[:, None] == start_offsets[None, :]) & (
            local_pos[:, None] >= local_pos[None, :]
        )
        normed_one, inverse_one, scaled_one = rms_parts(rows_in, attn_scale)
        first_hidden = scaled_one.astype(jnp.bfloat16)
        query_raw = jnp.dot(first_hidden, query_full, preferred_element_type=jnp.float32).reshape(
            tok_rows, local_heads, HEAD_SIZE
        )
        key_raw = jnp.dot(first_hidden, key_full, preferred_element_type=jnp.float32).reshape(
            tok_rows, local_groups, HEAD_SIZE
        )
        query_rot = rotate_half(query_raw, cosine_lookup, sine_lookup, 1.0).astype(jnp.bfloat16)
        key_rot = rotate_half(key_raw, cosine_lookup, sine_lookup, 1.0).astype(jnp.bfloat16)
        value_matrix_rows = (
            jnp.dot(first_hidden, value_full, preferred_element_type=jnp.float32)
            .astype(jnp.bfloat16)
            .reshape(tok_rows, local_groups, HEAD_SIZE)
        )
        grouped_queries = query_rot.reshape(tok_rows, local_groups, group_width, HEAD_SIZE)
        scores = masked_scores(grouped_queries, key_rot, allowed)
        top_score = jnp.max(scores, axis=-1, keepdims=True)
        expo = jnp.exp(scores - top_score)
        total = jnp.sum(expo, axis=-1, keepdims=True)
        log_total = top_score + jnp.log(total)
        probs_low = (expo / total).astype(jnp.bfloat16)
        attended = jnp.einsum(
            "kgqs,skd->qkgd", probs_low, value_matrix_rows, preferred_element_type=jnp.float32
        )
        attended = attended.reshape(tok_rows, local_heads * HEAD_SIZE).astype(jnp.bfloat16)
        branch_one = lax.psum(jnp.dot(attended, out_full, preferred_element_type=jnp.float32), "mp")
        after = rows_in + branch_one
        normed_two, inverse_two, scaled_two = rms_parts(after, mlp_scale)
        hidden_two = scaled_two.astype(jnp.bfloat16)
        gate_val = jnp.dot(hidden_two, gate_full, preferred_element_type=jnp.float32)
        up_val = jnp.dot(hidden_two, up_full, preferred_element_type=jnp.float32)
        sigmoid_gate = jax.nn.sigmoid(gate_val)
        activated = gate_val * sigmoid_gate
        mixed = (activated * up_val).astype(jnp.bfloat16)
        branch_two = lax.psum(jnp.dot(mixed, down_full, preferred_element_type=jnp.float32), "mp")
        outputs.append((after + branch_two).astype(jnp.bfloat16))
        gate_back, up_back, down_back, mlp_gain_back = (
            lax.all_gather(gate_weight, "dp", axis=0, tiled=True),
            lax.all_gather(up_weight, "dp", axis=0, tiled=True),
            lax.all_gather(down_weight, "dp", axis=1, tiled=True),
            lax.all_gather(mlp_gain, "dp", axis=0, tiled=True),
        )
        query_back, key_back, value_back, out_back, attn_gain_back = (
            lax.all_gather(query_weight, "dp", axis=0, tiled=True),
            lax.all_gather(key_matrix, "dp", axis=0, tiled=True),
            lax.all_gather(value_matrix, "dp", axis=0, tiled=True),
            lax.all_gather(out_weight, "dp", axis=1, tiled=True),
            lax.all_gather(attn_gain, "dp", axis=0, tiled=True),
        )
        grad_low = cotangent[batch_index]
        acc_down = acc_down + jnp.einsum(
            "tf,td->fd", mixed, grad_low, preferred_element_type=jnp.float32
        )
        grad_mixed = jnp.einsum(
            "td,fd->tf", grad_low, down_back, preferred_element_type=jnp.float32
        )
        grad_gate_act = (
            grad_mixed * up_val * (sigmoid_gate * (1.0 + gate_val * (1.0 - sigmoid_gate)))
        ).astype(jnp.bfloat16)
        grad_up_act = (grad_mixed * activated).astype(jnp.bfloat16)
        acc_gate = acc_gate + jnp.einsum(
            "td,tf->df", hidden_two, grad_gate_act, preferred_element_type=jnp.float32
        )
        acc_up = acc_up + jnp.einsum(
            "td,tf->df", hidden_two, grad_up_act, preferred_element_type=jnp.float32
        )
        grad_two_part = jnp.einsum(
            "tf,df->td", grad_gate_act, gate_back, preferred_element_type=jnp.float32
        )
        grad_two_part = grad_two_part + jnp.einsum(
            "tf,df->td", grad_up_act, up_back, preferred_element_type=jnp.float32
        )
        grad_hidden_two = lax.psum(grad_two_part, "mp")
        grad_norm_two, gain_two_term = rms_back(grad_hidden_two, normed_two, inverse_two, mlp_scale)
        acc_mlp_gain = acc_mlp_gain + gain_two_term
        grad_after = grad_low.astype(jnp.float32) + grad_norm_two
        grad_branch = grad_after.astype(jnp.bfloat16)
        acc_out = acc_out + jnp.einsum(
            "tc,td->cd", attended, grad_branch, preferred_element_type=jnp.float32
        )
        grad_attended = jnp.einsum(
            "td,cd->tc", grad_branch, out_back, preferred_element_type=jnp.float32
        ).astype(jnp.bfloat16)
        grad_attended = grad_attended.reshape(tok_rows, local_groups, group_width, HEAD_SIZE)
        probs_full = jnp.exp(masked_scores(grouped_queries, key_rot, allowed) - log_total)
        grad_probs = jnp.einsum(
            "qkgd,skd->kgqs", grad_attended, value_matrix_rows, preferred_element_type=jnp.float32
        )
        row_inner = jnp.sum(probs_full * grad_probs, axis=-1, keepdims=True)
        grad_scores = (probs_full * (grad_probs - row_inner)).astype(jnp.bfloat16)
        grad_query_rot = (
            jnp.einsum("kgqs,skd->qkgd", grad_scores, key_rot, preferred_element_type=jnp.float32)
            * score_scale
        )
        grad_key_rot = (
            jnp.einsum(
                "kgqs,qkgd->skd", grad_scores, grouped_queries, preferred_element_type=jnp.float32
            )
            * score_scale
        )
        grad_value_rows = jnp.einsum(
            "kgqs,qkgd->skd",
            probs_full.astype(jnp.bfloat16),
            grad_attended,
            preferred_element_type=jnp.float32,
        )
        grad_queries = rotate_half(
            grad_query_rot.reshape(tok_rows, local_heads, HEAD_SIZE),
            cosine_lookup,
            sine_lookup,
            -1.0,
        )
        grad_queries = grad_queries.reshape(tok_rows, local_heads * HEAD_SIZE).astype(jnp.bfloat16)
        grad_keys = (
            rotate_half(grad_key_rot, cosine_lookup, sine_lookup, -1.0)
            .reshape(tok_rows, local_groups * HEAD_SIZE)
            .astype(jnp.bfloat16)
        )
        grad_values = grad_value_rows.reshape(tok_rows, local_groups * HEAD_SIZE).astype(
            jnp.bfloat16
        )
        acc_query = acc_query + jnp.einsum(
            "td,tc->dc", first_hidden, grad_queries, preferred_element_type=jnp.float32
        )
        acc_key = acc_key + jnp.einsum(
            "td,tc->dc", first_hidden, grad_keys, preferred_element_type=jnp.float32
        )
        acc_value = acc_value + jnp.einsum(
            "td,tc->dc", first_hidden, grad_values, preferred_element_type=jnp.float32
        )
        grad_one_part = jnp.einsum(
            "tc,dc->td", grad_queries, query_back, preferred_element_type=jnp.float32
        )
        grad_one_part = grad_one_part + jnp.einsum(
            "tc,dc->td", grad_keys, key_back, preferred_element_type=jnp.float32
        )
        grad_one_part = grad_one_part + jnp.einsum(
            "tc,dc->td", grad_values, value_back, preferred_element_type=jnp.float32
        )
        grad_hidden_one = lax.psum(grad_one_part, "mp")
        grad_norm_one, gain_one_term = rms_back(
            grad_hidden_one, normed_one, inverse_one, attn_scale
        )
        acc_attn_gain = acc_attn_gain + gain_one_term
        input_grads.append(grad_after + grad_norm_one)
    attn_grads = (
        lax.psum_scatter(acc_attn_gain, "dp", scatter_dimension=0, tiled=True),
        lax.psum_scatter(acc_query, "dp", scatter_dimension=0, tiled=True),
        lax.psum_scatter(acc_key, "dp", scatter_dimension=0, tiled=True),
        lax.psum_scatter(acc_value, "dp", scatter_dimension=0, tiled=True),
        lax.psum_scatter(acc_out, "dp", scatter_dimension=1, tiled=True),
    )
    feed_grads = (
        lax.psum_scatter(acc_mlp_gain, "dp", scatter_dimension=0, tiled=True),
        lax.psum_scatter(acc_gate, "dp", scatter_dimension=0, tiled=True),
        lax.psum_scatter(acc_up, "dp", scatter_dimension=0, tiled=True),
        lax.psum_scatter(acc_down, "dp", scatter_dimension=1, tiled=True),
    )
    return (
        jnp.stack(outputs),
        jnp.stack(input_grads),
        attn_grads[0],
        attn_grads[1],
        attn_grads[2],
        attn_grads[3],
        attn_grads[4],
        feed_grads[0],
        feed_grads[1],
        feed_grads[2],
        feed_grads[3],
    )


def solution(mesh):
    in_specs = (
        P(None, "dp", None),
        P(None, "dp"),
        P(None, "dp", None),
        P("dp"),
        P("dp", "mp"),
        P("dp", "mp"),
        P("dp", "mp"),
        P("mp", "dp"),
        P("dp"),
        P("dp", "mp"),
        P("dp", "mp"),
        P("mp", "dp"),
    )
    out_specs = (
        P(None, "dp", None),
        P(None, "dp", None),
        P("dp"),
        P("dp", "mp"),
        P("dp", "mp"),
        P("dp", "mp"),
        P("mp", "dp"),
        P("dp"),
        P("dp", "mp"),
        P("dp", "mp"),
        P("mp", "dp"),
    )
    return jax.shard_map(
        per_device, mesh=mesh, in_specs=in_specs, out_specs=out_specs, check_vma=False
    )
```

profile of v0, /device:TPU:0, one launch (start us, length us, event | category | flops | bytes accessed | tf_op | source)
XLA Modules:
  0.0 2486.1 jit_solution(4314345725623328528)
XLA Ops:
  10.0 23.2 all-gather
  38.2 12.7 all-gather.12.cloned.1.call-done
  53.7 36.2 %all-gather.10.cloned.1.call-done = bf16[2048,256]{1,0:T(8,128)(2,1)} async-done(((bf16[128,256]{1,0:T(8,128)(2,1)}), bf16[2048,256]{1,0:T(8,128)(2,1)}) %all-gather.10.cloned.1.call-update) | async-done | bytes 1048592 | tf_op jit(solution)/shard_map/all_gather | solution.py:86
  93.3 48.3 %all-gather.14.cloned.1.call-done = bf16[2048,1024]{1,0:T(8,128)(2,1)} async-done(((bf16[128,1024]{1,0:T(8,128)(2,1)}), bf16[2048,1024]{1,0:T(8,128)(2,1)}) %all-gather.14.cloned.1.call-update) | async-done | bytes 4194320 | tf_op jit(solution)/shard_map/all_gather | solution.py:84
  141.6 6.4 copy.50
  148.0 3.9 fusion.85
  159.2 36.1 %all-gather.16.cloned.1.call-done = bf16[1024,2048]{1,0:T(8,128)(2,1)} async-done(((bf16[1024,128]{1,0:T(8,128)(2,1)}), bf16[1024,2048]{1,0:T(8,128)(2,1)}) %all-gather.16.cloned.1.call-update) | async-done | bytes 4194320 | tf_op jit(solution)/shard_map/all_gather | solution.py:87
  195.3 4.9 fusion.152
  205.0 18.6 all-gather.1
  223.6 85.8 %all-reduce.14.cloned.1.call-done = (f32[256,2048]{1,0:T(8,128)}, f32[256,2048]{1,0:T(8,128)}) async-done(((f32[256,2048]{1,0:T(8,128)}, f32[256,2048]{1,0:T(8,128)}), (f32[256,2048]{1,0:T(8,128)}, f32[256,2048]{1,0:T(8,128)})) %all-reduce.14.cloned.1.call-update) | async-done | bytes 4194320 | tf_op jit(solution)/shard_map/psum | solution.py:133
  309.4 2.8 multiply_reduce_fusion.5
  314.7 123.9 %all-gather.18.cloned.1.call-done = bf16[2048,4096]{1,0:T(8,128)(2,1)} async-done(((bf16[128,4096]{1,0:T(8,128)(2,1)}), bf16[2048,4096]{1,0:T(8,128)(2,1)}) %all-gather.18.cloned.1.call-update) | async-done | bytes 16777232 | tf_op jit(solution)/shard_map/all_gather | solution.py:91
  438.6 10.1 fusion.153
  448.8 117.3 %all-gather.20.cloned.1.call-done = bf16[2048,4096]{1,0:T(8,128)(2,1)} async-done(((bf16[128,4096]{1,0:T(8,128)(2,1)}), bf16[2048,4096]{1,0:T(8,128)(2,1)}) %all-gather.20.cloned.1.call-update) | async-done | bytes 16777232 | tf_op jit(solution)/shard_map/all_gather | solution.py:92
  566.1 10.5 fusion.154
  578.9 6.2 fusion.149
  585.1 10.3 fusion.150
  595.4 101.6 %all-gather.22.cloned.1.call-done = bf16[4096,2048]{1,0:T(8,128)(2,1)} async-done(((bf16[4096,128]{1,0:T(8,128)(2,1)}), bf16[4096,2048]{1,0:T(8,128)(2,1)}) %all-gather.22.cloned.1.call-update) | async-done | bytes 16777232 | tf_op jit(solution)/shard_map/all_gather | solution.py:93
  697.0 13.0 multiply_convert_fusion
  710.0 12.2 fusion.158
  722.3 12.8 multiply_convert_fusion.2
  735.1 12.5 fusion.156
  747.6 10.6 convolution_add_fusion.11
  758.1 12.9 convolution_add_fusion.12
  772.6 10.3 fusion.155
  782.9 10.2 fusion.151
  793.1 84.5 %all-reduce.12.cloned.1.call-done = (f32[256,2048]{1,0:T(8,128)}, f32[256,2048]{1,0:T(8,128)}) async-done(((f32[256,2048]{1,0:T(8,128)}, f32[256,2048]{1,0:T(8,128)}), (f32[256,2048]{1,0:T(8,128)}, f32[256,2048]{1,0:T(8,128)})) %all-reduce.12.cloned.1.call-update) | async-done | bytes 4194320 | tf_op jit(solution)/shard_map/psum | solution.py:180
  877.6 4.6 multiply_reduce_fusion.1
  888.0 3.3 fusion
  898.9 3.3 fusion.3
  932.3 4.8 convolution_add_fusion.4
  938.1 3.0 fusion.112
  941.2 4.7 convolution_add_fusion.3
  947.1 15.4 fusion.160
  962.5 25.2 %convolution_add_fusion.2 = f32[2048,4096]{1,0:T(8,128)} fusion(f32[2048,4096]{1,0:T(8,128)} %fusion.160, bf16[256,2048]{1,0:T(8,128)(2,1)S(1)} %copy-done.19, bf16[256,4096]{1,0:T(8,128)(2,1)S(1)} %copy-done.42), kind=kOutput, calls=%fused_computation.2 | convolution fusion | flops 4303355904 | bytes 70254592 | tf_op jit(solution)/shard_map/td,tf->df/dot_general | solution.py:168
  987.8 15.1 fusion.161
  1002.9 25.8 %convolution_add_fusion.1 = f32[2048,4096]{1,0:T(8,128)} fusion(f32[2048,4096]{1,0:T(8,128)} %fusion.161, bf16[256,2048]{1,0:T(8,128)(2,1)S(1)} %copy-done.20, bf16[256,4096]{1,0:T(8,128)(2,1)S(1)} %copy-done.41), kind=kOutput, calls=%fused_computation.1 | convolution fusion | flops 4303355904 | bytes 70254592 | tf_op jit(solution)/shard_map/td,tf->df/dot_general | solution.py:171
  1029.0 18.6 fusion.81
  1047.6 22.7 convolution_add_fusion
  1072.2 47.7 %all-reduce.10.cloned.1.call-done = (f32[256,2048]{1,0:T(8,128)}, f32[256,2048]{1,0:T(8,128)}, f32[256,2048]{1,0:T(8,128)}, f32[256,2048]{1,0:T(8,128)}) async-done(((f32[256,2048]{1,0:T(8,128)}, f32[256,2048]{1,0:T(8,128)}, f32[256,2048]{1,0:T(8,128)}, f32[256,2048]{1,0:T(8,128)}), (f32[256,2048]{1,0:T(8,128)}, f32[256,2048]{1,0:T(8,128)}, f32[256,2048]{1,0:T(8,128)}, ...) | async-done | bytes 8388624 | tf_op jit(solution)/shard_map/psum | solution.py:142
  1120.0 3.3 fusion.32
  1123.3 61.7 %all-reduce.2 = (f32[2048]{0:T(1024)S(1)}, f32[2048]{0:T(1024)S(1)}) all-reduce(f32[2048]{0:T(1024)S(1)} %add.244, f32[2048]{0:T(1024)S(1)} %add.251), channel_id=2, replica_groups=mesh['dp'=16,'mp'=2] {'dp'}, use_global_device_ids=true, to_apply=%region_24.25.clone | all-reduce | flops 4096 | bytes 32768
  1197.5 54.0 %reduce-scatter.12.cloned.1.call-done = f32[128,256]{1,0:T(8,128)} async-done(((f32[2048,256]{1,0:T(8,128)}), f32[128,256]{1,0:T(8,128)}) %reduce-scatter.12.cloned.1.call-update) | async-done | bytes 131088 | tf_op jit(solution)/shard_map/reduce_scatter | solution.py:257
  1251.5 108.3 %reduce-scatter.8.cloned.1.call-done = f32[128,1024]{1,0:T(8,128)} async-done(((f32[2048,1024]{1,0:T(8,128)}), f32[128,1024]{1,0:T(8,128)}) %reduce-scatter.8.cloned.1.call-update) | async-done | bytes 524304 | tf_op jit(solution)/shard_map/reduce_scatter | solution.py:255
  1359.8 109.1 %reduce-scatter.14.cloned.1.call-done = f32[1024,128]{1,0:T(8,128)} async-done(((f32[1024,2048]{1,0:T(8,128)}), f32[1024,128]{1,0:T(8,128)}) %reduce-scatter.14.cloned.1.call-update) | async-done | bytes 524304 | tf_op jit(solution)/shard_map/reduce_scatter | solution.py:258
  1469.0 337.1 %reduce-scatter.16.cloned.1.call-done = f32[128,4096]{1,0:T(8,128)} async-done(((f32[2048,4096]{1,0:T(8,128)}), f32[128,4096]{1,0:T(8,128)}) %reduce-scatter.16.cloned.1.call-update) | async-done | bytes 2097168 | tf_op jit(solution)/shard_map/reduce_scatter | solution.py:262
  1806.1 336.5 %reduce-scatter.18.cloned.1.call-done = f32[128,4096]{1,0:T(8,128)} async-done(((f32[2048,4096]{1,0:T(8,128)}), f32[128,4096]{1,0:T(8,128)}) %reduce-scatter.18.cloned.1.call-update) | async-done | bytes 2097168 | tf_op jit(solution)/shard_map/reduce_scatter | solution.py:263
  2142.7 336.5 %reduce-scatter.20.cloned.1.call-done = f32[4096,128]{1,0:T(8,128)} async-done(((f32[4096,2048]{1,0:T(8,128)}), f32[4096,128]{1,0:T(8,128)}) %reduce-scatter.20.cloned.1.call-update) | async-done | bytes 2097168 | tf_op jit(solution)/shard_map/reduce_scatter | solution.py:264
  (293 shorter events, 91.5 us)
Async XLA Ops:
  7.2 43.7 %all-gather.12.cloned.1.call-start = ((), (), s32[]{:S(2)}) async-start(), calls=%async_computation.8 | async-start | bytes 1114112 | tf_op jit(solution)/shard_map/all_gather | solution.py:85
  7.9 82.0 %all-gather.10.cloned.1.call-start = ((), (), s32[]{:S(2)}) async-start(), calls=%async_computation.7 | async-start | bytes 1114112 | tf_op jit(solution)/shard_map/all_gather | solution.py:86
  8.7 132.9 %all-gather.14.cloned.1.call-start = ((), (), s32[]{:S(2)}) async-start(), calls=%async_computation.9 | async-start | bytes 4456448 | tf_op jit(solution)/shard_map/all_gather | solution.py:84
  9.4 185.9 %all-gather.16.cloned.1.call-start = ((), (), s32[]{:S(2)}) async-start(), calls=%async_computation.10 | async-start | bytes 4456448 | tf_op jit(solution)/shard_map/all_gather | solution.py:87
  10.0 299.5 %all-reduce.14.cloned.1.call-start = ((), (), s32[]{:S(2)}) async-start(), calls=%async_computation.23 | async-start | bytes 8388608 | tf_op jit(solution)/shard_map/psum | solution.py:133
  33.2 118.8 %copy-start.59 = (f32[16,1,128]{2,1,0:T(1,128)}, f32[16,1,128]{2,1,0:T(1,128)S(1)}, u32[]{:S(2)}) copy-start(f32[16,1,128]{2,1,0:T(1,128)S(1)} %convert_element_type.294) | copy-start | bytes 24580
  34.9 118.6 %copy-start.57 = (f32[256,64]{0,1:T(8,128)}, f32[256,64]{0,1:T(8,128)S(1)}, u32[]{:S(2)}) copy-start(f32[256,64]{0,1:T(8,128)S(1)} %get-tuple-element.76) | copy-start | bytes 196612
  35.7 118.1 %copy-start.55 = (f32[256,64]{0,1:T(8,128)}, f32[256,64]{0,1:T(8,128)S(1)}, u32[]{:S(2)}) copy-start(f32[256,64]{0,1:T(8,128)S(1)} %get-tuple-element.72) | copy-start | bytes 196612
  35.7 16.7 copy-start
  38.0 110.0 %copy-start.75 = (f32[256]{0:T(256)}, f32[256]{0:T(256)S(1)}, u32[]{:S(2)}) copy-start(f32[256]{0:T(256)S(1)} %get-tuple-element.101) | copy-start | bytes 3076
  38.0 114.0 %copy-start.73 = (f32[256]{0:T(256)}, f32[256]{0:T(256)S(1)}, u32[]{:S(2)}) copy-start(f32[256]{0:T(256)S(1)} %get-tuple-element.102) | copy-start | bytes 3076
  53.6 100.4 %copy-start.46 = (bf16[256,4,64,1]{0,2,3,1:T(8,128)(2,1)}, bf16[256,4,64,1]{0,2,3,1:T(8,128)(2,1)S(1)}, u32[]{:S(2)}) copy-start(bf16[256,4,64,1]{0,2,3,1:T(8,128)(2,1)S(1)} %fusion.127) | copy-start | bytes 393220
  53.7 101.8 %copy-start.44 = (bf16[256,4,64,1]{0,2,3,1:T(8,128)(2,1)}, bf16[256,4,64,1]{0,2,3,1:T(8,128)(2,1)S(1)}, u32[]{:S(2)}) copy-start(bf16[256,4,64,1]{0,2,3,1:T(8,128)(2,1)S(1)} %fusion.128) | copy-start | bytes 393220
  91.9 65.0 %copy-start.71 = (bf16[256,256]{0,1:T(8,128)(2,1)}, bf16[256,256]{0,1:T(8,128)(2,1)S(1)}, u32[]{:S(2)}) copy-start(bf16[256,256]{0,1:T(8,128)(2,1)S(1)} %convolution_convert_fusion.2) | copy-start | bytes 393220
  148.0 4.0 copy-start.34
  157.8 37.6 %copy-start.67 = (bf16[4,64,4,256]{3,1,2,0:T(8,128)(2,1)}, bf16[4,64,4,256]{3,1,2,0:T(8,128)(2,1)S(1)}, u32[]{:S(2)}) copy-start(bf16[4,64,4,256]{3,1,2,0:T(8,128)(2,1)S(1)} %fusion.54) | copy-start | bytes 1572868
  159.2 41.1 %copy-start.61 = (bf16[4,64,4,256]{3,1,2,0:T(8,128)(2,1)}, bf16[4,64,4,256]{3,1,2,0:T(8,128)(2,1)S(1)}, u32[]{:S(2)}) copy-start(bf16[4,64,4,256]{3,1,2,0:T(8,128)(2,1)S(1)} %fusion.55) | copy-start | bytes 1572868
  195.3 4.9 copy-start.81
  202.9 235.7 %all-gather.18.cloned.1.call-start = ((), (), s32[]{:S(2)}) async-start(), calls=%async_computation.11 | async-start | bytes 17825792 | tf_op jit(solution)/shard_map/all_gather | solution.py:91
  203.5 362.6 %all-gather.20.cloned.1.call-start = ((), (), s32[]{:S(2)}) async-start(), calls=%async_computation.12 | async-start | bytes 17825792 | tf_op jit(solution)/shard_map/all_gather | solution.py:92
  204.2 492.8 %all-gather.22.cloned.1.call-start = ((), (), s32[]{:S(2)}) async-start(), calls=%async_computation.13 | async-start | bytes 17825792 | tf_op jit(solution)/shard_map/all_gather | solution.py:93
  205.0 672.6 %all-reduce.12.cloned.1.call-start = ((), (), s32[]{:S(2)}) async-start(), calls=%async_computation.22 | async-start | bytes 8388608 | tf_op jit(solution)/shard_map/psum | solution.py:180
  314.7 251.4 %copy-start.18 = (bf16[256,2048]{1,0:T(8,128)(2,1)}, bf16[256,2048]{1,0:T(8,128)(2,1)S(1)}, u32[]{:S(2)}) copy-start(bf16[256,2048]{1,0:T(8,128)(2,1)S(1)} %get-tuple-element.80) | copy-start | bytes 3145732
  314.7 270.4 %copy-start.16 = (bf16[256,2048]{1,0:T(8,128)(2,1)}, bf16[256,2048]{1,0:T(8,128)(2,1)S(1)}, u32[]{:S(2)}) copy-start(bf16[256,2048]{1,0:T(8,128)(2,1)S(1)} %get-tuple-element.79) | copy-start | bytes 3145732
  566.1 12.8 copy-start.80
  585.1 111.9 %copy-start.22 = (bf16[2,256,2048]{2,1,0:T(8,128)(2,1)S(1)}, bf16[2,256,2048]{2,1,0:T(8,128)(2,1)}, u32[]{:S(2)}) copy-start(bf16[2,256,2048]{2,1,0:T(8,128)(2,1)} %param.14) | copy-start | bytes 6291460
  735.1 12.5 copy-start.40
  771.0 348.9 %all-reduce.10.cloned.1.call-start = ((), (), s32[]{:S(2)}) async-start(), calls=%async_computation.21 | async-start | bytes 16777216 | tf_op jit(solution)/shard_map/psum | solution.py:142
  772.6 10.3 copy-start.38
  782.9 94.7 %copy-start.7 = (f32[256,2048]{1,0:T(8,128)S(1)}, f32[256,2048]{1,0:T(8,128)}, u32[]{:S(2)}) copy-start(f32[256,2048]{1,0:T(8,128)} %copy-done.6) | copy-start | bytes 6291460
  877.6 4.6 copy-start.10
  877.6 4.6 copy-start.23
  877.6 4.7 copy-start.25
  877.6 5.3 copy-start.26
  912.1 5.8 copy-start.48
  920.2 277.3 %reduce-scatter.10.cloned.1.call-start = ((), (), s32[]{:S(2)}) async-start(), calls=%async_computation.15 | async-start | bytes 2228224 | tf_op jit(solution)/shard_map/reduce_scatter | solution.py:256
  925.4 326.1 %reduce-scatter.12.cloned.1.call-start = ((), (), s32[]{:S(2)}) async-start(), calls=%async_computation.16 | async-start | bytes 2228224 | tf_op jit(solution)/shard_map/reduce_scatter | solution.py:257
  928.1 431.8 %reduce-scatter.8.cloned.1.call-start = ((), (), s32[]{:S(2)}) async-start(), calls=%async_computation.14 | async-start | bytes 8912896 | tf_op jit(solution)/shard_map/reduce_scatter | solution.py:255
  937.1 4.0 copy-start.68
  937.1 531.9 %reduce-scatter.14.cloned.1.call-start = ((), (), s32[]{:S(2)}) async-start(), calls=%async_computation.17 | async-start | bytes 8912896 | tf_op jit(solution)/shard_map/reduce_scatter | solution.py:258
  945.9 860.2 %reduce-scatter.16.cloned.1.call-start = ((), (), s32[]{:S(2)}) async-start(), calls=%async_computation.18 | async-start | bytes 35651584 | tf_op jit(solution)/shard_map/reduce_scatter | solution.py:262
  947.1 15.4 copy-start.19
  947.1 15.4 copy-start.42
  987.8 1154.9 %reduce-scatter.18.cloned.1.call-start = ((), (), s32[]{:S(2)}) async-start(), calls=%async_computation.19 | async-start | bytes 35651584 | tf_op jit(solution)/shard_map/reduce_scatter | solution.py:263
  987.8 15.1 copy-start.20
  987.8 15.1 copy-start.41
  1028.7 1450.4 %reduce-scatter.20.cloned.1.call-start = ((), (), s32[]{:S(2)}) async-start(), calls=%async_computation.20 | async-start | bytes 35651584 | tf_op jit(solution)/shard_map/reduce_scatter | solution.py:264
  1029.0 18.6 copy-start.24
  (54 other events, 99.6 us)
Sparse Core Ops, SparseCore 0:
  10.2 40.6 all-gather.11
  53.0 36.8 all-gather.9
  92.1 49.4 all-gather.13
  143.6 51.6 all-gather.15
  203.0 106.3 all-reduce.13
  311.7 126.8 all-gather.17
  441.0 125.0 all-gather.19
  568.4 128.5 all-gather.21
  771.1 106.3 all-reduce.11
  920.3 199.5 all-reduce.9
  1124.3 61.9 reduce-scatter.9
  1190.9 60.5 reduce-scatter.11
  1256.1 103.6 reduce-scatter.7
  1364.3 104.5 reduce-scatter.13
  1473.7 332.4 reduce-scatter.15
  1810.8 331.8 reduce-scatter.17
  2147.3 331.7 reduce-scatter.19
where the time goes:
time: 2500 us; the launch traced here: 2490 us
  waiting for transfers between devices  1980 us (79%)
  matrix products  318 us (13%)
  blocking collectives  103 us (4%)
  other arithmetic  33.9 us (1%)
  local copies, waits for them, and re-layouts  33 us (1%)
    reduce_scatter x1, waiting for transfers between devices, per_device(): lax.psum_scatter(acc_gate, 'dp', scatter_dimension=0, tiled=True)  337 us
    reduce_scatter x1, waiting for transfers between devices, per_device(): lax.psum_scatter(acc_up, 'dp', scatter_dimension=0, tiled=True)  337 us
    reduce_scatter x1, waiting for transfers between devices, per_device(): lax.psum_scatter(acc_down, 'dp', scatter_dimension=1, tiled=True)  336 us
    all_gather x1, waiting for transfers between devices, per_device(): lax.all_gather(gate_weight, 'dp', axis=0, tiled=True)  124 us
    all_gather x1, waiting for transfers between devices, per_device(): lax.all_gather(up_weight, 'dp', axis=0, tiled=True)  117 us
    reduce_scatter x1, waiting for transfers between devices, per_device(): lax.psum_scatter(acc_out, 'dp', scatter_dimension=1, tiled=True)  109 us
    reduce_scatter x1, waiting for transfers between devices, per_device(): lax.psum_scatter(acc_query, 'dp', scatter_dimension=0, tiled=True)  108 us
    all_gather x1, waiting for transfers between devices, per_device(): lax.all_gather(down_weight, 'dp', axis=1, tiled=True)  102 us
  transfers between devices with their start and end apart: 17, of which 16 were waited for; matrix products, arithmetic and copies ran while one was open for 10% of the time, Pallas kernels for 0%

commit v1 on v0

v1 whole, which is shorter than its diff:
```python
import math

import jax
import jax.numpy as jnp
from jax import lax
from jax.sharding import PartitionSpec as P

HEAD_SIZE = 64
EPSILON = 1e-05
F32 = jnp.float32
BF16 = jnp.bfloat16


def rms_parts(values_in, gain):
    inverse = lax.rsqrt(jnp.mean(values_in * values_in, axis=-1, keepdims=True) + EPSILON)
    normed = values_in * inverse
    return (normed, inverse, normed * gain)


def rms_back(grad_scaled, normed, inverse, gain):
    grad_normed = grad_scaled * gain
    inner_mean = jnp.mean(grad_normed * normed, axis=-1, keepdims=True)
    return inverse * (grad_normed - normed * inner_mean)


def rope_tables(positions, head_dim):
    halfway = head_dim // 2
    frequency = 500000.0 ** (-(jnp.arange(halfway, dtype=F32) * 2.0 / head_dim))
    angles = positions.astype(F32)[..., None] * frequency
    angles = jnp.concatenate([angles, angles], axis=-1)
    return (jnp.cos(angles), jnp.sin(angles))


def rotate_half(head_rows, cosine_lookup, sine_lookup, direction):
    halfway = head_rows.shape[-1] // 2
    turned = jnp.concatenate([-head_rows[..., halfway:], head_rows[..., :halfway]], axis=-1)
    return head_rows * cosine_lookup[..., None, :] + direction * turned * sine_lookup[..., None, :]


def dot(left, right, left_dim, right_dim):
    return lax.dot_general(
        left, right, (((left_dim,), (right_dim,)), ((), ())), preferred_element_type=F32
    )


def add_low(left, right):
    return (left.astype(F32) + right.astype(F32)).astype(BF16)


def make_per_device(n):
    pair = 4 if n <= 16 else 8
    others = [1 << b for b in reversed(range(n.bit_length() - 1)) if (1 << b) != pair]
    main_order = [pair] + others
    other_order = [v for v in others[::-1] if v not in (1, pair)] + [pair, 1]

    def swap(array, bit):
        return lax.ppermute(array, "dp", [(i, i ^ bit) for i in range(n)])

    def swap_mp(array):
        return lax.ppermute(array, "mp", [(0, 1), (1, 0)])

    def per_device(
        inputs,
        seq_starts,
        cotangent,
        attn_gain,
        query_weight,
        key_matrix,
        value_matrix,
        out_weight,
        mlp_gain,
        gate_weight,
        up_weight,
        down_weight,
    ):
        micro_count, rows, width = inputs.shape
        block = width // n
        tokens = micro_count * rows
        q_cols, k_cols = query_weight.shape[1], key_matrix.shape[1]
        local_heads, local_groups = q_cols // HEAD_SIZE, k_cols // HEAD_SIZE
        group_width = local_heads // local_groups
        score_scale = 1.0 / math.sqrt(HEAD_SIZE)
        me, mine = lax.axis_index("dp"), lax.axis_index("mp")
        low = (me // pair) % 2
        is_low = low == 0

        def place_of(position):
            index = jnp.int32(0)
            for axis, bit in enumerate(main_order):
                digit = (position >> axis) & 1
                if bit == pair:
                    index = index + digit * bit
                else:
                    index = index + (((me // bit) % 2 + digit) % 2) * bit
            return index

        def position_of(index):
            position = jnp.int32(0)
            for axis, bit in enumerate(main_order):
                digit = 1 if index & bit else 0
                if bit == pair:
                    position = position + (digit << axis)
                else:
                    position = position + (((me // bit) % 2 + digit) % 2) * (1 << axis)
            return position

        def to_relative(array):
            pieces = [
                lax.dynamic_slice_in_dim(array, place_of(p) * block, block, array.ndim - 1)
                for p in range(n)
            ]
            return jnp.concatenate(pieces, axis=-1)

        def from_relative(array):
            pieces = [
                lax.dynamic_slice_in_dim(array, position_of(j) * block, block, array.ndim - 1)
                for j in range(n)
            ]
            return jnp.concatenate(pieces, axis=-1)

        def own_first(array):
            return jnp.stack(
                [
                    lax.dynamic_index_in_dim(array, mine, 0, False),
                    lax.dynamic_index_in_dim(array, 1 - mine, 0, False),
                ]
            )

        def micro_order(array):
            return jnp.stack(
                [
                    lax.dynamic_index_in_dim(array, mine, 0, False),
                    lax.dynamic_index_in_dim(array, 1 - mine, 0, False),
                ]
            )

        def paired(array, other):
            return jnp.stack(
                [jnp.where(is_low, array, other), jnp.where(is_low, other, array)]
            )

        def gather_whole(shard, order):
            array, axes = shard, []
            for bit in order:
                other = swap(array, bit)
                array = paired(array, other) if bit == pair else jnp.stack([array, other])
                axes = [bit] + axes
            wanted = main_order[::-1]
            array = array.transpose([axes.index(b) for b in wanted] + [len(axes), len(axes) + 1])
            return array.reshape(width, shard.shape[1])

        def gather_half(shard):
            half = shard.shape[1] // 2
            keep = lax.dynamic_slice_in_dim(shard, low * half, half, 1)
            send = lax.dynamic_slice_in_dim(shard, (1 - low) * half, half, 1)
            array = paired(keep, swap(send, pair)).reshape(2 * block, half)
            for bit in others:
                array = jnp.concatenate([array, swap(array, bit)], axis=0)
            return array

        def first_stage(left, right):
            middle = width // 2
            send = dot(left[:, middle:], right, 0, 0).astype(BF16)
            other = swap(send, 1)
            return (dot(left[:, :middle], right, 0, 0) + other.astype(F32)).astype(BF16)

        def scatter_whole(array, order):
            columns = array.shape[1]
            bits = main_order[:-1][::-1]
            array = array.reshape([2] * len(bits) + [block, columns])
            left = list(bits)
            for bit in [b for b in order[::-1] if b != 1]:
                axis = left.index(bit)
                if bit == pair:
                    keep = lax.dynamic_index_in_dim(array, low, axis, False)
                    send = lax.dynamic_index_in_dim(array, 1 - low, axis, False)
                else:
                    keep = lax.index_in_dim(array, 0, axis, False)
                    send = lax.index_in_dim(array, 1, axis, False)
                array = add_low(keep, swap(send, bit))
                left.pop(axis)
            return array

        def scatter_half(array):
            for bit in others[::-1]:
                if bit == 1:
                    continue
                middle = array.shape[0] // 2
                array = add_low(array[:middle], swap(array[middle:], bit))
            array = array.reshape(2, block, array.shape[1])
            keep = lax.dynamic_index_in_dim(array, low, 0, False)
            other = swap(lax.dynamic_index_in_dim(array, 1 - low, 0, False), pair)
            return jnp.where(
                is_low,
                jnp.concatenate([keep, other], axis=1),
                jnp.concatenate([other, keep], axis=1),
            ).astype(F32)

        def gather_gains(shards):
            array = shards
            for bit in main_order:
                other = swap(array, bit)
                array = paired(array, other) if bit == pair else jnp.stack([array, other])
            array = array.reshape(n, shards.shape[0], block)
            return array.transpose(1, 0, 2).reshape(shards.shape[0], width)

        def scatter_gain(gradient):
            array = gradient.reshape([2] * len(main_order) + [block])
            array = array + swap_mp(array)
            for bit in main_order[::-1]:
                if bit == pair:
                    keep = lax.dynamic_index_in_dim(array, low, 0, False)
                    send = lax.dynamic_index_in_dim(array, 1 - low, 0, False)
                else:
                    keep, send = array[0], array[1]
                array = keep + swap(send, bit)
            return array

        def gather_square(own):
            middle = rows // 2
            by_mp, by_pair = swap_mp(own), swap(own, pair)
            first = swap_mp(by_pair[:middle])
            second = swap(by_mp[middle:], pair)
            return jnp.concatenate([own, by_mp, by_pair, first, second], axis=0)

        def scatter_square(own, by_mp, by_pair, both):
            middle = rows // 2
            first = swap(both[:middle], pair)
            second = swap_mp(both[middle:])
            to_mp = jnp.concatenate([add_low(by_mp[:middle], first), by_mp[middle:]], axis=0)
            to_pair = jnp.concatenate([by_pair[:middle], add_low(by_pair[middle:], second)], axis=0)
            return own.astype(F32) + swap_mp(to_mp).astype(F32) + swap(to_pair, pair).astype(F32)

        attn_low = jnp.concatenate([query_weight, key_matrix, value_matrix], axis=1)
        half_cols = attn_low.shape[1] // 2
        gains = gather_gains(jnp.stack([attn_gain, mlp_gain])).astype(F32)
        attn_scale, mlp_scale = gains[0], gains[1]
        qkv_full = jnp.concatenate(
            [
                gather_whole(attn_low[:, :half_cols], main_order),
                gather_whole(attn_low[:, half_cols:], other_order),
            ],
            axis=1,
        )
        out_full = gather_whole(out_weight.T, main_order)
        gate_full = gather_half(gate_weight)
        up_full = gather_half(up_weight)
        down_full = gather_half(down_weight.T)

        cot = to_relative(own_first(cotangent))
        cot_pair = swap(cot[0], pair)
        cot_both = swap_mp(cot_pair)
        cot_all = jnp.concatenate([cot[0], cot[1], cot_pair, cot_both], axis=0)

        rows_in = to_relative(own_first(inputs)).astype(F32).reshape(tokens, width)
        starts = own_first(seq_starts)
        local_pos = jnp.arange(rows, dtype=jnp.int32)
        positions = me * rows + local_pos[None] - starts
        cosine_lookup, sine_lookup = rope_tables(positions.reshape(tokens), HEAD_SIZE)
        allowed = (starts[:, :, None] == starts[:, None, :]) & (
            local_pos[:, None] >= local_pos[None, :]
        )
        normed_one, inverse_one, scaled_one = rms_parts(rows_in, attn_scale)
        first_hidden = scaled_one.astype(BF16)
        qkv = dot(first_hidden, qkv_full, 1, 0)
        query_raw = qkv[:, :q_cols].reshape(tokens, local_heads, HEAD_SIZE)
        key_raw = qkv[:, q_cols : q_cols + k_cols].reshape(tokens, local_groups, HEAD_SIZE)
        query_rot = rotate_half(query_raw, cosine_lookup, sine_lookup, 1.0).astype(BF16)
        key_rot = rotate_half(key_raw, cosine_lookup, sine_lookup, 1.0).astype(BF16)
        key_rot = key_rot.reshape(micro_count, rows, local_groups, HEAD_SIZE)
        value_rows = (
            qkv[:, q_cols + k_cols :]
            .astype(BF16)
            .reshape(micro_count, rows, local_groups, HEAD_SIZE)
        )
        grouped = query_rot.reshape(micro_count, rows, local_groups, group_width, HEAD_SIZE)
        scores = (
            jnp.einsum("bqkgd,bskd->bkgqs", grouped, key_rot, preferred_element_type=F32)
            * score_scale
        )
        scores = jnp.where(allowed[:, None, None], scores, -1e30)
        expo = jnp.exp(scores - jnp.max(scores, axis=-1, keepdims=True))
        probs = expo / jnp.sum(expo, axis=-1, keepdims=True)
        probs_low = probs.astype(BF16)
        attended = jnp.einsum(
            "bkgqs,bskd->bqkgd", probs_low, value_rows, preferred_element_type=F32
        )
        attended = attended.reshape(tokens, q_cols).astype(BF16)
        branch_other = dot(attended[rows:], out_full, 1, 1).astype(BF16)
        branch_own = dot(attended[:rows], out_full, 1, 1)
        after = rows_in[:rows] + branch_own + swap_mp(branch_other).astype(F32)

        normed_two, inverse_two, scaled_two = rms_parts(after, mlp_scale)
        hidden_two = gather_square(scaled_two.astype(BF16))
        gate_val = dot(hidden_two, gate_full, 1, 0)
        up_val = dot(hidden_two, up_full, 1, 0)
        sigmoid_gate = jax.nn.sigmoid(gate_val)
        activated = gate_val * sigmoid_gate
        mixed = (activated * up_val).astype(BF16)
        grad_down = first_stage(cot_all, mixed)

        grad_mixed = dot(cot_all, down_full, 1, 0)
        grad_gate_act = (
            grad_mixed * up_val * (sigmoid_gate * (1.0 + gate_val * (1.0 - sigmoid_gate)))
        ).astype(BF16)
        grad_up_act = (grad_mixed * activated).astype(BF16)
        grad_two = (dot(grad_gate_act, gate_full, 1, 1) + dot(grad_up_act, up_full, 1, 1)).astype(
            BF16
        )
        grad_two = grad_two.reshape(4, rows, width)
        grad_hidden_two = scatter_square(*[grad_two[i] for i in range(4)])
        grad_gate = first_stage(hidden_two, grad_gate_act)
        grad_up = first_stage(hidden_two, grad_up_act)

        branch_two = dot(mixed, down_full, 1, 1).astype(BF16).reshape(4, rows, width)
        result = (after + scatter_square(*[branch_two[i] for i in range(4)])).astype(BF16)
        output = from_relative(micro_order(jnp.stack([result, swap_mp(result)])))

        gain_two = jnp.sum(grad_hidden_two * normed_two, axis=0)
        grad_after = cot[0].astype(F32) + rms_back(
            grad_hidden_two, normed_two, inverse_two, mlp_scale
        )
        grad_branch_own = grad_after.astype(BF16)
        grad_branch = jnp.concatenate([grad_branch_own, swap_mp(grad_branch_own)], axis=0)

        grad_out = first_stage(grad_branch, attended)
        grad_attended = dot(grad_branch, out_full, 1, 0).astype(BF16)
        grad_attended = grad_attended.reshape(
            micro_count, rows, local_groups, group_width, HEAD_SIZE
        )
        grad_probs = jnp.einsum(
            "bqkgd,bskd->bkgqs", grad_attended, value_rows, preferred_element_type=F32
        )
        row_inner = jnp.sum(probs * grad_probs, axis=-1, keepdims=True)
        grad_scores = (probs * (grad_probs - row_inner)).astype(BF16)
        grad_query_rot = (
            jnp.einsum("bkgqs,bskd->bqkgd", grad_scores, key_rot, preferred_element_type=F32)
            * score_scale
        )
        grad_key_rot = (
            jnp.einsum("bkgqs,bqkgd->bskd", grad_scores, grouped, preferred_element_type=F32)
            * score_scale
        )
        grad_value_rows = jnp.einsum(
            "bkgqs,bqkgd->bskd", probs_low, grad_attended, preferred_element_type=F32
        )
        grad_queries = rotate_half(
            grad_query_rot.reshape(tokens, local_heads, HEAD_SIZE),
            cosine_lookup,
            sine_lookup,
            -1.0,
        ).reshape(tokens, q_cols)
        grad_keys = rotate_half(
            grad_key_rot.reshape(tokens, local_groups, HEAD_SIZE),
            cosine_lookup,
            sine_lookup,
            -1.0,
        ).reshape(tokens, k_cols)
        grad_qkv = jnp.concatenate(
            [
                grad_queries.astype(BF16),
                grad_keys.astype(BF16),
                grad_value_rows.reshape(tokens, k_cols).astype(BF16),
            ],
            axis=1,
        )
        grad_one_part = dot(grad_qkv, qkv_full, 1, 1).astype(BF16)
        one_other = swap_mp(grad_one_part)
        one_other = jnp.concatenate([one_other[rows:], one_other[:rows]], axis=0)
        grad_hidden_one = grad_one_part.astype(F32) + one_other.astype(F32)
        grad_attn_low = first_stage(first_hidden, grad_qkv)
        grad_after_all = jnp.concatenate([grad_branch[:rows], grad_branch[rows:]], axis=0)
        input_grad = grad_after_all.astype(F32) + rms_back(
            grad_hidden_one, normed_one, inverse_one, attn_scale
        )
        input_grad = from_relative(micro_order(input_grad.reshape(micro_count, rows, width)))
        gain_one = jnp.sum(grad_one_part.astype(F32) * normed_one, axis=0)

        grad_down = scatter_half(grad_down)
        grad_gate = scatter_half(grad_gate)
        grad_up = scatter_half(grad_up)
        grad_out = scatter_whole(grad_out, main_order).astype(F32)
        grad_attn = jnp.concatenate(
            [
                scatter_whole(grad_attn_low[:, :half_cols], main_order),
                scatter_whole(grad_attn_low[:, half_cols:], other_order),
            ],
            axis=1,
        ).astype(F32)
        return (
            output,
            input_grad,
            scatter_gain(gain_one),
            grad_attn[:, :q_cols],
            grad_attn[:, q_cols : q_cols + k_cols],
            grad_attn[:, q_cols + k_cols :],
            grad_out.T,
            scatter_gain(gain_two),
            grad_gate,
            grad_up,
            grad_down.T,
        )

    return per_device


def solution(mesh):
    in_specs = (
        P(None, "dp", None),
        P(None, "dp"),
        P(None, "dp", None),
        P("dp"),
        P("dp", "mp"),
        P("dp", "mp"),
        P("dp", "mp"),
        P("mp", "dp"),
        P("dp"),
        P("dp", "mp"),
        P("dp", "mp"),
        P("mp", "dp"),
    )
    out_specs = (
        P(None, "dp", None),
        P(None, "dp", None),
        P("dp"),
        P("dp", "mp"),
        P("dp", "mp"),
        P("dp", "mp"),
        P("mp", "dp"),
        P("dp"),
        P("dp", "mp"),
        P("dp", "mp"),
        P("mp", "dp"),
    )
    return jax.shard_map(
        make_per_device(mesh.shape["dp"]),
        mesh=mesh,
        in_specs=in_specs,
        out_specs=out_specs,
        check_vma=False,
    )
```

time: 2500 us -> 1020 us (0.41)
  waiting for transfers between devices: 1980 us -> 494 us
  matrix products: 318 us -> 174 us
  blocking collectives: 103 us -> 0 us
  starting transfers between devices: 1.49 us -> 100 us
  other arithmetic: 33.9 us -> 124 us
  local copies, waits for them, and re-layouts: 33 us -> 114 us
    reduce_scatter x7 -> x0, waiting for transfers between devices: 1280 us -> none  [the longest x1 337 us: per_device(): lax.psum_scatter(acc_gate, 'dp', scatter_dimension=0, tiled=True)]
    ppermute x0 -> x79, waiting for transfers between devices: none -> 494 us  [the longest x66 471 us: swap(): return lax.ppermute(array, 'dp', [(i, i ^ bit) for i in range(n)])]
    all_gather x7 -> x0, waiting for transfers between devices: 476 us -> none  [the longest x1 124 us: per_device(): lax.all_gather(gate_weight, 'dp', axis=0, tiled=True)]
    psum x3 -> x0, waiting for transfers between devices: 218 us -> none  [the longest x1 85.8 us: per_device(): lax.psum(jnp.dot(attended, out_full, preferred_element_type=jnp.float32),...]
    dot_general x54 -> x27, matrix products: 318 us -> 174 us  [the longest x21 156 us: dot(): lax.dot_general(left, right, (((left_dim,), (right_dim,)), ((), ())), pre...]
    ppermute x0 -> x79, starting transfers between devices: none -> 100 us  [the longest x66 84.1 us: swap(): return lax.ppermute(array, 'dp', [(i, i ^ bit) for i in range(n)])]
    unnamed x1 -> x0, blocking collectives: 61.7 us -> none
    all_gather x2 -> x0, blocking collectives: 41.7 us -> none  [the longest x1 23.2 us: per_device(): lax.all_gather(attn_gain, 'dp', axis=0, tiled=True)]
  transfers between devices with their start and end apart: 17 -> 79, of which waited for: 16 -> 37; matrix products, arithmetic and copies ran while one was open for 10% -> 33% of each run, Pallas kernels for 0% -> 0%
where the time goes in v1:
time: 1020 us; the launch traced here: 1010 us
  waiting for transfers between devices  494 us (48%)
  matrix products  174 us (17%)
  other arithmetic  124 us (12%)
  local copies, waits for them, and re-layouts  114 us (11%)
  starting transfers between devices  100 us (10%)
    ppermute x66, waiting for transfers between devices, swap(): return lax.ppermute(array, 'dp', [(i, i ^ bit) for i in range(n)])  471 us
    dot_general x21, matrix products, dot(): lax.dot_general(left, right, (((left_dim,), (right_dim,)), ((), ())), pre...  156 us
    ppermute x66, starting transfers between devices, swap(): return lax.ppermute(array, 'dp', [(i, i ^ bit) for i in range(n)])  84.1 us
    unnamed x228, local copies, waits for them, and re-layouts  44.8 us
    unnamed x62, other arithmetic  28.3 us
    ppermute x13, waiting for transfers between devices, swap_mp(): return lax.ppermute(array, 'mp', [(0, 1), (1, 0)])  22.3 us
  transfers between devices with their start and end apart: 79, of which 37 were waited for; matrix products, arithmetic and copies ran while one was open for 33% of the time, Pallas kernels for 0%

profile of v1, /device:TPU:0, one launch (start us, length us, event | category | flops | bytes accessed | tf_op | source)
XLA Modules:
  0.0 1009.3 jit_solution(18140322408767747576)
XLA Ops:
  85.6 8.4 collective-permute-done.5
  97.6 39.4 %collective-permute-done.9 = bf16[2,128,768]{2,1,0:T(8,128)(2,1)S(1)} collective-permute-done((bf16[2,128,768]{2,1,0:T(8,128)(2,1)S(1)}, bf16[2,128,768]{2,1,0:T(8,128)(2,1)S(1)}, u32[]{:S(2)}, u32[]{:S(2)}) %collective-permute-start.9) | collective-permute-done | bytes 393248 | tf_op jit(solution)/shard_map/ppermute | solution.py:57
  137.0 22.6 %collective-permute-start.6 = (bf16[2,2,128,768]{3,2,1,0:T(8,128)(2,1)S(1)}, bf16[2,2,128,768]{3,2,1,0:T(8,128)(2,1)S(1)}, u32[]{:S(2)}, u32[]{:S(2)}) collective-permute-start(bf16[2,2,128,768]{3,2,1,0:T(8,128)(2,1)S(1)} %get-tuple-element.137), channel_id=1, source_target_pairs={{0,4},{2,6},{4,0},{6,2},{8,12},{10,14},{12,8},{14,10},{16,20},{18,... | collective-permute-start | bytes 2359304 | tf_op jit(solution)/shard_map/ppermute | solution.py:57
  167.7 10.3 %collective-permute-done.6 = bf16[2,2,128,768]{3,2,1,0:T(8,128)(2,1)S(1)} collective-permute-done((bf16[2,2,128,768]{3,2,1,0:T(8,128)(2,1)S(1)}, bf16[2,2,128,768]{3,2,1,0:T(8,128)(2,1)S(1)}, u32[]{:S(2)}, u32[]{:S(2)}) %collective-permute-start.6) | collective-permute-done | bytes 786464 | tf_op jit(solution)/shard_map/ppermute | solution.py:57
  178.3 15.5 %collective-permute-done.10 = bf16[2,2,128,768]{3,2,0,1:T(8,128)(2,1)S(1)} collective-permute-done((bf16[2,2,128,768]{3,2,0,1:T(8,128)(2,1)S(1)}, bf16[2,2,128,768]{3,2,0,1:T(8,128)(2,1)S(1)}, u32[]{:S(2)}, u32[]{:S(2)}) %collective-permute-start.10) | collective-permute-done | bytes 786464 | tf_op jit(solution)/shard_map/ppermute | solution.py:57
  197.5 7.0 collective-permute-done.22
  206.7 18.9 %collective-permute-done.26 = bf16[256,2048]{1,0:T(8,128)(2,1)S(1)} collective-permute-done((bf16[256,2048]{1,0:T(8,128)(2,1)S(1)}, bf16[256,2048]{1,0:T(8,128)(2,1)S(1)}, u32[]{:S(2)}, u32[]{:S(2)}) %collective-permute-start.26) | collective-permute-done | bytes 1048608 | tf_op jit(solution)/shard_map/ppermute | solution.py:57
  265.8 4.5 fusion.235
  271.7 4.3 fusion.46
  290.2 31.0 %collective-permute-done.27 = bf16[512,2048]{1,0:T(8,128)(2,1)} collective-permute-done((bf16[512,2048]{1,0:T(8,128)(2,1)}, bf16[512,2048]{1,0:T(8,128)(2,1)}, u32[]{:S(2)}, u32[]{:S(2)}) %collective-permute-start.27) | collective-permute-done | bytes 2097184 | tf_op jit(solution)/shard_map/ppermute | solution.py:57
  321.2 3.8 pad_maximum_fusion.6
  328.9 4.1 collective-permute-start.18
  335.5 3.7 pad_maximum_fusion.8
  341.5 15.6 %collective-permute-done.18 = bf16[256,2048]{1,0:T(8,128)(2,1)} collective-permute-done((bf16[256,2048]{1,0:T(8,128)(2,1)}, bf16[256,2048]{1,0:T(8,128)(2,1)}, u32[]{:S(2)}, u32[]{:S(2)}) %collective-permute-start.18) | collective-permute-done | bytes 1048608 | tf_op jit(solution)/shard_map/ppermute | solution.py:57
  359.7 4.0 collective-permute-done.31
  366.3 3.8 collective-permute-start.20
  372.0 10.7 %collective-permute-done.20 = bf16[128,2048]{1,0:T(8,128)(2,1)S(1)} collective-permute-done((bf16[128,2048]{1,0:T(8,128)(2,1)S(1)}, bf16[128,2048]{1,0:T(8,128)(2,1)S(1)}, u32[]{:S(2)}, u32[]{:S(2)}) %collective-permute-start.20) | collective-permute-done | bytes 524320 | tf_op jit(solution)/shard_map/ppermute | solution.py:57
  382.8 14.5 %fusion.45 = f32[1024,2048]{1,0:T(8,128)} fusion(bf16[1024,2048]{1,0:T(8,128)(2,1)S(1)} %constant_dynamic-update-slice_fusion.32, bf16[1024,2048]{1,0:T(8,128)(2,1)} %collective-permute-done.24, bf16[512,2048]{1,0:T(8,128)(2,1)} %collective-permute-done.23, bf16[256,2048]{1,0:T(8,128)(2,1)S(1)} %copy-done.30, bf16[256,2048]{1,0:T(8,128)(2,1)S(1)} %bitcast.374), kind=kOutput, calls=%fused_computation.249 | convolution fusion | flops 8623489024 | bytes 20971520 | tf_op jit(solution)/shard_map/dot_general | solution.py:41
  397.3 13.1 %fusion.44 = f32[1024,2048]{1,0:T(8,128)} fusion(bf16[1024,2048]{1,0:T(8,128)(2,1)S(1)} %constant_dynamic-update-slice_fusion.32, bf16[1024,2048]{1,0:T(8,128)(2,1)} %collective-permute-done.28, bf16[512,2048]{1,0:T(8,128)(2,1)} %collective-permute-done.27, bf16[256,2048]{1,0:T(8,128)(2,1)S(1)} %copy-done.34, bf16[256,2048]{1,0:T(8,128)(2,1)S(1)} %bitcast.379), kind=kOutput, calls=%fused_computation.248 | convolution fusion | flops 8623489024 | bytes 20971520 | tf_op jit(solution)/shard_map/dot_general | solution.py:41
  410.4 20.1 %multiply_convert_fusion.1 = (bf16[1024,2048]{1,0:T(8,128)(2,1)}, bf16[1024,2048]{1,0:T(8,128)(2,1)}, bf16[1024,2048]{1,0:T(8,128)(2,1)}) fusion(f32[1024,2048]{1,0:T(8,128)} %fusion.45, f32[1024,2048]{1,0:T(8,128)} %fusion.44, bf16[1024,2048]{1,0:T(8,128)(2,1)} %collective-permute-done.32, bf16[512,2048]{1,0:T(8,128)(2,1)} %collective-permute-done.31, ...), kind=kOutput, calls=%fused_computation.47 | convolution fusion | flops 8671723520 | bytes 41943040 | tf_op jit(solution)/shard_map/dot_general | solution.py:41
  430.5 14.8 %fusion.43 = f32[1024,2048]{1,0:T(8,128)} fusion(bf16[1024,2048]{1,0:T(8,128)(2,1)} %get-tuple-element.72, bf16[1024,2048]{1,0:T(8,128)(2,1)} %collective-permute-done.28, bf16[512,2048]{1,0:T(8,128)(2,1)} %collective-permute-done.27, bf16[256,2048]{1,0:T(8,128)(2,1)} %copy-done.32, bf16[256,2048]{1,0:T(8,128)(2,1)S(1)} %bitcast.380), kind=kOutput, calls=%fused_computation.247 | convolution fusion | flops 8623489024 | bytes 20971520 | tf_op jit(solution)/shard_map/dot_general | solution.py:41
  445.3 15.7 %add_convert_fusion.3 = bf16[1024,2048]{1,0:T(8,128)(2,1)} fusion(f32[1024,2048]{1,0:T(8,128)} %fusion.43, bf16[1024,2048]{1,0:T(8,128)(2,1)} %get-tuple-element.71, bf16[1024,2048]{1,0:T(8,128)(2,1)} %collective-permute-done.24, bf16[512,2048]{1,0:T(8,128)(2,1)} %collective-permute-done.23, bf16[256,2048]{1,0:T(8,128)(2,1)S(1)} %copy-done.31, ...), kind=kOutput, calls=%fused_computation.45 | convolution fusion | flops 8627683328 | bytes 25165824 | tf_op jit(solution)/shard_map/dot_general | solution.py:41
  466.9 13.4 %convolution_convert_fusion.1 = bf16[1024,2048]{1,0:T(8,128)(2,1)S(1)} fusion(bf16[1024,2048]{1,0:T(8,128)(2,1)} %get-tuple-element.73, bf16[1024,2048]{1,0:T(8,128)(2,1)} %collective-permute-done.32, bf16[512,2048]{1,0:T(8,128)(2,1)} %collective-permute-done.31, bf16[256,2048]{1,0:T(8,128)(2,1)} %collective-permute-done.30, bf16[256,2048]{1,0:T(8,128)(2,1)} %bitcast.81), kind=kOutput, calls=%fused_computation.182 | convolution fusion | flops 8625586176 | bytes 16777216 | tf_op jit(solution)/shard_map/dot_general | solution.py:41
  482.5 8.7 convolution_convert_fusion.4
  494.1 6.2 convolution_convert_fusion.3
  501.1 16.3 %collective-permute-done.43 = bf16[256,2048]{1,0:T(8,128)(2,1)S(1)} collective-permute-done((bf16[256,2048]{1,0:T(8,128)(2,1)S(1)}, bf16[256,2048]{1,0:T(8,128)(2,1)S(1)}, u32[]{:S(2)}, u32[]{:S(2)}) %collective-permute-start.43) | collective-permute-done | bytes 1048608 | tf_op jit(solution)/shard_map/ppermute | solution.py:57
  528.4 16.3 %collective-permute-done.36 = bf16[256,2048]{1,0:T(8,128)(2,1)S(1)} collective-permute-done((bf16[256,2048]{1,0:T(8,128)(2,1)S(1)}, bf16[256,2048]{1,0:T(8,128)(2,1)S(1)}, u32[]{:S(2)}, u32[]{:S(2)}) %collective-permute-start.36) | collective-permute-done | bytes 1048608 | tf_op jit(solution)/shard_map/ppermute | solution.py:57
  544.8 3.9 collective-permute-done.34
  553.4 6.5 convolution_convert_fusion.2
  562.1 15.6 %collective-permute-done.44 = bf16[256,2048]{1,0:T(8,128)(2,1)S(1)} collective-permute-done((bf16[256,2048]{1,0:T(8,128)(2,1)S(1)}, bf16[256,2048]{1,0:T(8,128)(2,1)S(1)}, u32[]{:S(2)}, u32[]{:S(2)}) %collective-permute-start.44) | collective-permute-done | bytes 1048608 | tf_op jit(solution)/shard_map/ppermute | solution.py:60
  582.0 4.1 reshape.376
  588.8 5.2 fusion.56
  594.0 4.9 fusion.1
  634.0 6.8 add_convert_fusion.2
  645.2 6.7 add_convert_fusion.1
  656.3 6.6 add_convert_fusion
  666.3 4.3 fusion.16
  671.5 5.2 fusion.13
  688.0 49.6 %collective-permute-done.48 = f32[2,2,128]{2,1,0:T(2,128)S(1)} collective-permute-done((f32[2,2,128]{2,1,0:T(2,128)S(1)}, f32[2,2,128]{2,1,0:T(2,128)S(1)}, u32[]{:S(2)}, u32[]{:S(2)}) %collective-permute-start.48) | collective-permute-done | bytes 2080 | tf_op jit(solution)/shard_map/ppermute | solution.py:57
  746.8 13.3 %collective-permute-done.59 = bf16[2,2,128,1024]{2,3,1,0:T(8,128)(2,1)} collective-permute-done((bf16[2,2,128,1024]{2,3,1,0:T(8,128)(2,1)}, bf16[2,2,128,1024]{2,3,1,0:T(8,128)(2,1)}, u32[]{:S(2)}, u32[]{:S(2)}) %collective-permute-start.59) | collective-permute-done | bytes 1048608 | tf_op jit(solution)/shard_map/ppermute | solution.py:57
  762.0 3.8 add_convert_fusion.4
  766.7 20.2 %collective-permute-done.60 = bf16[2,128,1024]{1,2,0:T(8,128)(2,1)S(1)} collective-permute-done((bf16[2,128,1024]{1,2,0:T(8,128)(2,1)S(1)}, bf16[2,128,1024]{1,2,0:T(8,128)(2,1)S(1)}, u32[]{:S(2)}, u32[]{:S(2)}) %collective-permute-start.60) | collective-permute-done | bytes 524320 | tf_op jit(solution)/shard_map/ppermute | solution.py:57
  795.0 9.9 collective-permute-done.76
  807.3 14.1 %collective-permute-done.52 = bf16[2,2,128,768]{3,2,1,0:T(8,128)(2,1)S(1)} collective-permute-done((bf16[2,2,128,768]{3,2,1,0:T(8,128)(2,1)S(1)}, bf16[2,2,128,768]{3,2,1,0:T(8,128)(2,1)S(1)}, u32[]{:S(2)}, u32[]{:S(2)}) %collective-permute-start.52) | collective-permute-done | bytes 786464 | tf_op jit(solution)/shard_map/ppermute | solution.py:57
  826.1 128.9 %collective-permute-done.53 = bf16[2,128,768]{2,1,0:T(8,128)(2,1)S(1)} collective-permute-done((bf16[2,128,768]{2,1,0:T(8,128)(2,1)S(1)}, bf16[2,128,768]{2,1,0:T(8,128)(2,1)S(1)}, u32[]{:S(2)}, u32[]{:S(2)}) %collective-permute-start.53) | collective-permute-done | bytes 393248 | tf_op jit(solution)/shard_map/ppermute | solution.py:57
  955.2 7.0 collective-permute-done.56
  989.8 8.0 collective-permute-done.74
  1001.0 5.3 collective-permute-done.78
  (611 shorter events, 329.4 us)
Async XLA Ops:
  1.9 60.9 %collective-permute-start = (bf16[2,128]{1,0:T(2,128)(2,1)}, bf16[2,128]{1,0:T(2,128)(2,1)}, u32[]{:S(2)}, u32[]{:S(2)}) collective-permute-start(bf16[2,128]{1,0:T(2,128)(2,1)} %pad_maximum_fusion.52), channel_id=1, source_target_pairs={{0,8},{2,10},{4,12},{6,14},{8,0},{10,2},{12,4},{14,6},{16,24},{18,... | collective-permute-start | bytes 1544 | tf_op jit(solution)/shard_map/ppermute | solution.py:57
  6.6 66.6 %collective-permute-start.4 = (bf16[128,768]{1,0:T(8,128)(2,1)}, bf16[128,768]{1,0:T(8,128)(2,1)}, u32[]{:S(2)}, u32[]{:S(2)}) collective-permute-start(bf16[128,768]{1,0:T(8,128)(2,1)} %slice.320), channel_id=1, source_target_pairs={{0,8},{2,10},{4,12},{6,14},{8,0},{10,2},{12,4},{14,6},{16,24},{18,... | collective-permute-start | bytes 589832 | tf_op jit(solution)/shard_map/ppermute | solution.py:57
  8.4 67.8 %collective-permute-start.12 = (bf16[128,1024]{1,0:T(8,128)(2,1)}, bf16[128,1024]{1,0:T(8,128)(2,1)}, u32[]{:S(2)}, u32[]{:S(2)}) collective-permute-start(bf16[128,1024]{1,0:T(8,128)(2,1)} %bitcast.58), channel_id=1, source_target_pairs={{0,8},{2,10},{4,12},{6,14},{8,0},{10,2},{12,4},{14,6},{16,24},{18,... | collective-permute-start | bytes 786440 | tf_op jit(solution)/shard_map/ppermute | solution.py:57
  12.3 71.7 %collective-permute-start.21 = (bf16[128,2048]{1,0:T(8,128)(2,1)}, bf16[128,2048]{1,0:T(8,128)(2,1)}, u32[]{:S(2)}, u32[]{:S(2)}) collective-permute-start(bf16[128,2048]{1,0:T(8,128)(2,1)} %constant_dynamic-slice_fusion.19), channel_id=1, source_target_pairs={{0,8},{2,10},{4,12},{6,14},{8,0},{10,2},{12,4},{14,6},{16,24},{18,... | collective-permute-start | bytes 1572872 | tf_op jit(solution)/shard_map/ppermute | solution.py:57
  14.1 145.5 %collective-permute-start.29 = (bf16[128,2048]{1,0:T(8,128)(2,1)}, bf16[128,2048]{1,0:T(8,128)(2,1)}, u32[]{:S(2)}, u32[]{:S(2)}) collective-permute-start(bf16[128,2048]{1,0:T(8,128)(2,1)} %bitcast.78), channel_id=1, source_target_pairs={{0,8},{2,10},{4,12},{6,14},{8,0},{10,2},{12,4},{14,6},{16,24},{18,... | collective-permute-start | bytes 1572872 | tf_op jit(solution)/shard_map/ppermute | solution.py:57
  73.0 87.9 %collective-permute-start.25 = (bf16[128,2048]{1,0:T(8,128)(2,1)}, bf16[128,2048]{1,0:T(8,128)(2,1)S(1)}, u32[]{:S(2)}, u32[]{:S(2)}) collective-permute-start(bf16[128,2048]{1,0:T(8,128)(2,1)} %constant_dynamic-slice_fusion.18), channel_id=1, source_target_pairs={{0,8},{2,10},{4,12},{6,14},{8,0},{10,2},{12,4},{14,6},{16,24},{18,... | collective-permute-start | bytes 1572872 | tf_op jit(solution)/shard_map/ppermute | solution.py:57
  81.1 84.9 %collective-permute-start.13 = (bf16[2,128,1024]{2,1,0:T(8,128)(2,1)S(1)}, bf16[2,128,1024]{2,1,0:T(8,128)(2,1)S(1)}, u32[]{:S(2)}, u32[]{:S(2)}) collective-permute-start(bf16[2,128,1024]{2,1,0:T(8,128)(2,1)S(1)} %get-tuple-element.141), channel_id=1, source_target_pairs={{0,16},{2,18},{4,20},{6,22},{8,24},{10,26},{12,28},{14,30},{16,0},... | collective-permute-start | bytes 1572872 | tf_op jit(solution)/shard_map/ppermute | solution.py:57
  84.0 53.0 %collective-permute-start.9 = (bf16[2,128,768]{2,1,0:T(8,128)(2,1)S(1)}, bf16[2,128,768]{2,1,0:T(8,128)(2,1)S(1)}, u32[]{:S(2)}, u32[]{:S(2)}) collective-permute-start(bf16[2,128,768]{2,1,0:T(8,128)(2,1)S(1)} %get-tuple-element.153), channel_id=1, source_target_pairs={{0,16},{2,18},{4,20},{6,22},{8,24},{10,26},{12,28},{14,30},{16,0},... | collective-permute-start | bytes 1179656 | tf_op jit(solution)/shard_map/ppermute | solution.py:57
  94.0 110.5 %collective-permute-start.22 = (bf16[256,2048]{1,0:T(8,128)(2,1)S(1)}, bf16[256,2048]{1,0:T(8,128)(2,1)S(1)}, u32[]{:S(2)}, u32[]{:S(2)}) collective-permute-start(bf16[256,2048]{1,0:T(8,128)(2,1)S(1)} %bitcast.371), channel_id=1, source_target_pairs={{0,16},{2,18},{4,20},{6,22},{8,24},{10,26},{12,28},{14,30},{16,0},... | collective-permute-start | bytes 3145736 | tf_op jit(solution)/shard_map/ppermute | solution.py:57
  137.0 41.1 %collective-permute-start.6 = (bf16[2,2,128,768]{3,2,1,0:T(8,128)(2,1)S(1)}, bf16[2,2,128,768]{3,2,1,0:T(8,128)(2,1)S(1)}, u32[]{:S(2)}, u32[]{:S(2)}) collective-permute-start(bf16[2,2,128,768]{3,2,1,0:T(8,128)(2,1)S(1)} %get-tuple-element.137), channel_id=1, source_target_pairs={{0,4},{2,6},{4,0},{6,2},{8,12},{10,14},{12,8},{14,10},{16,20},{18,... | collective-permute-start | bytes 2359304 | tf_op jit(solution)/shard_map/ppermute | solution.py:57
  159.7 34.1 %collective-permute-start.10 = (bf16[2,2,128,768]{3,2,0,1:T(8,128)(2,1)S(1)}, bf16[2,2,128,768]{3,2,0,1:T(8,128)(2,1)S(1)}, u32[]{:S(2)}, u32[]{:S(2)}) collective-permute-start(bf16[2,2,128,768]{3,2,0,1:T(8,128)(2,1)S(1)} %pad_maximum_fusion.40), channel_id=1, source_target_pairs={{0,8},{2,10},{4,12},{6,14},{8,0},{10,2},{12,4},{14,6},{16,24},{18,... | collective-permute-start | bytes 2359304 | tf_op jit(solution)/shard_map/ppermute | solution.py:57
  162.5 63.1 %collective-permute-start.26 = (bf16[256,2048]{1,0:T(8,128)(2,1)S(1)}, bf16[256,2048]{1,0:T(8,128)(2,1)S(1)}, u32[]{:S(2)}, u32[]{:S(2)}) collective-permute-start(bf16[256,2048]{1,0:T(8,128)(2,1)S(1)} %bitcast.376), channel_id=1, source_target_pairs={{0,16},{2,18},{4,20},{6,22},{8,24},{10,26},{12,28},{14,30},{16,0},... | collective-permute-start | bytes 3145736 | tf_op jit(solution)/shard_map/ppermute | solution.py:57
  166.1 61.2 %collective-permute-start.14 = (bf16[2,2,128,1024]{3,2,1,0:T(8,128)(2,1)S(1)}, bf16[2,2,128,1024]{3,2,1,0:T(8,128)(2,1)S(1)}, u32[]{:S(2)}, u32[]{:S(2)}) collective-permute-start(bf16[2,2,128,1024]{3,2,1,0:T(8,128)(2,1)S(1)} %get-tuple-element.135), channel_id=1, source_target_pairs={{0,4},{2,6},{4,0},{6,2},{8,12},{10,14},{12,8},{14,10},{16,20},{18,... | collective-permute-start | bytes 3145736 | tf_op jit(solution)/shard_map/ppermute | solution.py:57
  178.2 51.8 %collective-permute-start.7 = (bf16[2,2,2,128,768]{4,3,2,1,0:T(8,128)(2,1)S(1)}, bf16[2,2,2,128,768]{4,3,2,1,0:T(8,128)(2,1)S(1)}, u32[]{:S(2)}, u32[]{:S(2)}) collective-permute-start(bf16[2,2,2,128,768]{4,3,2,1,0:T(8,128)(2,1)S(1)} %get-tuple-element.117), channel_id=1, source_target_pairs={{0,2},{2,0},{4,6},{6,4},{8,10},{10,8},{12,14},{14,12},{16,18},{18,... | collective-permute-start | bytes 4718600 | tf_op jit(solution)/shard_map/ppermute | solution.py:57
  194.1 37.9 %collective-permute-start.11 = (bf16[2,2,2,128,768]{4,3,0,1,2:T(8,128)(2,1)S(1)}, bf16[2,2,2,128,768]{4,3,0,1,2:T(8,128)(2,1)S(1)}, u32[]{:S(2)}, u32[]{:S(2)}) collective-permute-start(bf16[2,2,2,128,768]{4,3,0,1,2:T(8,128)(2,1)S(1)} %get-tuple-element.119), channel_id=1, source_target_pairs={{0,2},{2,0},{4,6},{6,4},{8,10},{10,8},{12,14},{14,12},{16,18},{18,... | collective-permute-start | bytes 4718600 | tf_op jit(solution)/shard_map/ppermute | solution.py:57
  204.5 78.0 %collective-permute-start.38 = (bf16[256,2048]{1,0:T(8,128)(2,1)}, bf16[256,2048]{1,0:T(8,128)(2,1)}, u32[]{:S(2)}, u32[]{:S(2)}) collective-permute-start(bf16[256,2048]{1,0:T(8,128)(2,1)} %get-tuple-element.99), channel_id=1, source_target_pairs={{0,8},{2,10},{4,12},{6,14},{8,0},{10,2},{12,4},{14,6},{16,24},{18,... | collective-permute-start | bytes 3145736 | tf_op jit(solution)/shard_map/ppermute | solution.py:57
  225.6 60.8 %collective-permute-start.30 = (bf16[256,2048]{1,0:T(8,128)(2,1)}, bf16[256,2048]{1,0:T(8,128)(2,1)}, u32[]{:S(2)}, u32[]{:S(2)}) collective-permute-start(bf16[256,2048]{1,0:T(8,128)(2,1)} %bitcast.81), channel_id=1, source_target_pairs={{0,16},{2,18},{4,20},{6,22},{8,24},{10,26},{12,28},{14,30},{16,0},... | collective-permute-start | bytes 3145736 | tf_op jit(solution)/shard_map/ppermute | solution.py:57
  227.3 55.7 %collective-permute-start.23 = (bf16[512,2048]{1,0:T(8,128)(2,1)}, bf16[512,2048]{1,0:T(8,128)(2,1)}, u32[]{:S(2)}, u32[]{:S(2)}) collective-permute-start(bf16[512,2048]{1,0:T(8,128)(2,1)} %pad_maximum_fusion.17), channel_id=1, source_target_pairs={{0,4},{2,6},{4,0},{6,2},{8,12},{10,14},{12,8},{14,10},{16,20},{18,... | collective-permute-start | bytes 6291464 | tf_op jit(solution)/shard_map/ppermute | solution.py:57
  230.1 91.1 %collective-permute-start.27 = (bf16[512,2048]{1,0:T(8,128)(2,1)}, bf16[512,2048]{1,0:T(8,128)(2,1)}, u32[]{:S(2)}, u32[]{:S(2)}) collective-permute-start(bf16[512,2048]{1,0:T(8,128)(2,1)} %pad_maximum_fusion.18), channel_id=1, source_target_pairs={{0,4},{2,6},{4,0},{6,2},{8,12},{10,14},{12,8},{14,10},{16,20},{18,... | collective-permute-start | bytes 6291464 | tf_op jit(solution)/shard_map/ppermute | solution.py:57
  232.0 44.1 %collective-permute-start.15 = (bf16[2,2,2,128,1024]{4,3,2,1,0:T(8,128)(2,1)}, bf16[2,2,2,128,1024]{4,3,2,1,0:T(8,128)(2,1)}, u32[]{:S(2)}, u32[]{:S(2)}) collective-permute-start(bf16[2,2,2,128,1024]{4,3,2,1,0:T(8,128)(2,1)} %get-tuple-element.105), channel_id=1, source_target_pairs={{0,2},{2,0},{4,6},{6,4},{8,10},{10,8},{12,14},{14,12},{16,18},{18,... | collective-permute-start | bytes 6291464 | tf_op jit(solution)/shard_map/ppermute | solution.py:57
  280.9 44.1 %collective-permute-start.16 = (bf16[256,2048]{1,0:T(8,128)(2,1)S(1)}, bf16[256,2048]{1,0:T(8,128)(2,1)S(1)}, u32[]{:S(2)}, u32[]{:S(2)}) collective-permute-start(bf16[256,2048]{1,0:T(8,128)(2,1)S(1)} %convolution_convert_fusion.5), channel_id=1, source_target_pairs={{0,1},{1,0},{2,3},{3,2},{4,5},{5,4},{6,7},{7,6},{8,9},{9,8},{10,11... | collective-permute-start | bytes 3145736 | tf_op jit(solution)/shard_map/ppermute | solution.py:60
  282.5 50.5 %collective-permute-start.39 = (bf16[256,2048]{1,0:T(8,128)(2,1)}, bf16[256,2048]{1,0:T(8,128)(2,1)}, u32[]{:S(2)}, u32[]{:S(2)}) collective-permute-start(bf16[256,2048]{1,0:T(8,128)(2,1)} %collective-permute-done.38), channel_id=1, source_target_pairs={{0,1},{1,0},{2,3},{3,2},{4,5},{5,4},{6,7},{7,6},{8,9},{9,8},{10,11... | collective-permute-start | bytes 3145736 | tf_op jit(solution)/shard_map/ppermute | solution.py:60
  286.5 96.3 %collective-permute-start.24 = (bf16[1024,2048]{1,0:T(8,128)(2,1)}, bf16[1024,2048]{1,0:T(8,128)(2,1)}, u32[]{:S(2)}, u32[]{:S(2)}) collective-permute-start(bf16[1024,2048]{1,0:T(8,128)(2,1)} %pad_maximum_fusion.5), channel_id=1, source_target_pairs={{0,2},{2,0},{4,6},{6,4},{8,10},{10,8},{12,14},{14,12},{16,18},{18,... | collective-permute-start | bytes 12582920 | tf_op jit(solution)/shard_map/ppermute | solution.py:57
  289.7 74.0 %collective-permute-start.31 = (bf16[512,2048]{1,0:T(8,128)(2,1)}, bf16[512,2048]{1,0:T(8,128)(2,1)}, u32[]{:S(2)}, u32[]{:S(2)}) collective-permute-start(bf16[512,2048]{1,0:T(8,128)(2,1)} %pad_maximum_fusion.19), channel_id=1, source_target_pairs={{0,4},{2,6},{4,0},{6,2},{8,12},{10,14},{12,8},{14,10},{16,20},{18,... | collective-permute-start | bytes 6291464 | tf_op jit(solution)/shard_map/ppermute | solution.py:57
  325.0 72.3 %collective-permute-start.28 = (bf16[1024,2048]{1,0:T(8,128)(2,1)}, bf16[1024,2048]{1,0:T(8,128)(2,1)}, u32[]{:S(2)}, u32[]{:S(2)}) collective-permute-start(bf16[1024,2048]{1,0:T(8,128)(2,1)} %pad_maximum_fusion.6), channel_id=1, source_target_pairs={{0,2},{2,0},{4,6},{6,4},{8,10},{10,8},{12,14},{14,12},{16,18},{18,... | collective-permute-start | bytes 12582920 | tf_op jit(solution)/shard_map/ppermute | solution.py:57
  328.9 28.2 %collective-permute-start.18 = (bf16[256,2048]{1,0:T(8,128)(2,1)}, bf16[256,2048]{1,0:T(8,128)(2,1)}, u32[]{:S(2)}, u32[]{:S(2)}) collective-permute-start(bf16[256,2048]{1,0:T(8,128)(2,1)} %get-tuple-element.38), channel_id=1, source_target_pairs={{0,8},{2,10},{4,12},{6,14},{8,0},{10,2},{12,4},{14,6},{16,24},{18,... | collective-permute-start | bytes 3145736 | tf_op jit(solution)/shard_map/ppermute | solution.py:57
  333.0 33.2 %collective-permute-start.17 = (bf16[256,2048]{1,0:T(8,128)(2,1)}, bf16[256,2048]{1,0:T(8,128)(2,1)S(1)}, u32[]{:S(2)}, u32[]{:S(2)}) collective-permute-start(bf16[256,2048]{1,0:T(8,128)(2,1)} %get-tuple-element.38), channel_id=1, source_target_pairs={{0,1},{1,0},{2,3},{3,2},{4,5},{5,4},{6,7},{7,6},{8,9},{9,8},{10,11... | collective-permute-start | bytes 3145736 | tf_op jit(solution)/shard_map/ppermute | solution.py:60
  366.1 44.3 %collective-permute-start.32 = (bf16[1024,2048]{1,0:T(8,128)(2,1)S(1)}, bf16[1024,2048]{1,0:T(8,128)(2,1)}, u32[]{:S(2)}, u32[]{:S(2)}) collective-permute-start(bf16[1024,2048]{1,0:T(8,128)(2,1)S(1)} %pad_maximum_fusion.7), channel_id=1, source_target_pairs={{0,2},{2,0},{4,6},{6,4},{8,10},{10,8},{12,14},{14,12},{16,18},{18,... | collective-permute-start | bytes 12582920 | tf_op jit(solution)/shard_map/ppermute | solution.py:57
  491.3 140.6 %collective-permute-start.67 = (bf16[1024,2048]{1,0:T(8,128)(2,1)}, bf16[1024,2048]{1,0:T(8,128)(2,1)}, u32[]{:S(2)}, u32[]{:S(2)}) collective-permute-start(bf16[1024,2048]{1,0:T(8,128)(2,1)} %convolution_convert_fusion.4), channel_id=1, source_target_pairs={{0,2},{2,0},{4,6},{6,4},{8,10},{10,8},{12,14},{14,12},{16,18},{18,... | collective-permute-start | bytes 12582920 | tf_op jit(solution)/shard_map/ppermute | solution.py:57
  500.4 143.5 %collective-permute-start.71 = (bf16[1024,2048]{1,0:T(8,128)(2,1)}, bf16[1024,2048]{1,0:T(8,128)(2,1)}, u32[]{:S(2)}, u32[]{:S(2)}) collective-permute-start(bf16[1024,2048]{1,0:T(8,128)(2,1)} %convolution_convert_fusion.3), channel_id=1, source_target_pairs={{0,2},{2,0},{4,6},{6,4},{8,10},{10,8},{12,14},{14,12},{16,18},{18,... | collective-permute-start | bytes 12582920 | tf_op jit(solution)/shard_map/ppermute | solution.py:57
  559.9 95.1 %collective-permute-start.75 = (bf16[1024,2048]{1,0:T(8,128)(2,1)}, bf16[1024,2048]{1,0:T(8,128)(2,1)}, u32[]{:S(2)}, u32[]{:S(2)}) collective-permute-start(bf16[1024,2048]{1,0:T(8,128)(2,1)} %convolution_convert_fusion.2), channel_id=1, source_target_pairs={{0,2},{2,0},{4,6},{6,4},{8,10},{10,8},{12,14},{14,12},{16,18},{18,... | collective-permute-start | bytes 12582920 | tf_op jit(solution)/shard_map/ppermute | solution.py:57
  560.0 64.9 %collective-permute-start.37 = (bf16[256,2048]{1,0:T(8,128)(2,1)}, bf16[256,2048]{1,0:T(8,128)(2,1)}, u32[]{:S(2)}, u32[]{:S(2)}) collective-permute-start(bf16[256,2048]{1,0:T(8,128)(2,1)} %get-tuple-element.97), channel_id=1, source_target_pairs={{0,1},{1,0},{2,3},{3,2},{4,5},{5,4},{6,7},{7,6},{8,9},{9,8},{10,11... | collective-permute-start | bytes 3145736 | tf_op jit(solution)/shard_map/ppermute | solution.py:60
  620.1 45.5 %collective-permute-start.45 = (bf16[512,2048]{1,0:T(8,128)(2,1)S(1)}, bf16[512,2048]{1,0:T(8,128)(2,1)S(1)}, u32[]{:S(2)}, u32[]{:S(2)}) collective-permute-start(bf16[512,2048]{1,0:T(8,128)(2,1)S(1)} %fusion.22), channel_id=1, source_target_pairs={{0,1},{1,0},{2,3},{3,2},{4,5},{5,4},{6,7},{7,6},{8,9},{9,8},{10,11... | collective-permute-start | bytes 6291464 | tf_op jit(solution)/shard_map/ppermute | solution.py:60
  624.9 137.1 %collective-permute-start.51 = (bf16[1024,1536]{1,0:T(8,128)(2,1)}, bf16[1024,1536]{1,0:T(8,128)(2,1)}, u32[]{:S(2)}, u32[]{:S(2)}) collective-permute-start(bf16[1024,1536]{1,0:T(8,128)(2,1)} %convolution_convert_fusion), channel_id=1, source_target_pairs={{0,2},{2,0},{4,6},{6,4},{8,10},{10,8},{12,14},{14,12},{16,18},{18,... | collective-permute-start | bytes 9437192 | tf_op jit(solution)/shard_map/ppermute | solution.py:57
  631.8 46.0 %collective-permute-start.58 = (bf16[1024,1024]{1,0:T(8,128)(2,1)S(1)}, bf16[1024,1024]{1,0:T(8,128)(2,1)S(1)}, u32[]{:S(2)}, u32[]{:S(2)}) collective-permute-start(bf16[1024,1024]{1,0:T(8,128)(2,1)S(1)} %convolution_convert_fusion.6), channel_id=1, source_target_pairs={{0,2},{2,0},{4,6},{6,4},{8,10},{10,8},{12,14},{14,12},{16,18},{18,... | collective-permute-start | bytes 6291464 | tf_op jit(solution)/shard_map/ppermute | solution.py:57
  643.9 143.7 %collective-permute-start.68 = (bf16[512,2048]{1,0:T(8,128)(2,1)}, bf16[512,2048]{1,0:T(8,128)(2,1)}, u32[]{:S(2)}, u32[]{:S(2)}) collective-permute-start(bf16[512,2048]{1,0:T(8,128)(2,1)} %slice.478), channel_id=1, source_target_pairs={{0,4},{2,6},{4,0},{6,2},{8,12},{10,14},{12,8},{14,10},{16,20},{18,... | collective-permute-start | bytes 6291464 | tf_op jit(solution)/shard_map/ppermute | solution.py:57
  655.0 135.3 %collective-permute-start.72 = (bf16[512,2048]{1,0:T(8,128)(2,1)}, bf16[512,2048]{1,0:T(8,128)(2,1)}, u32[]{:S(2)}, u32[]{:S(2)}) collective-permute-start(bf16[512,2048]{1,0:T(8,128)(2,1)} %slice.482), channel_id=1, source_target_pairs={{0,4},{2,6},{4,0},{6,2},{8,12},{10,14},{12,8},{14,10},{16,20},{18,... | collective-permute-start | bytes 6291464 | tf_op jit(solution)/shard_map/ppermute | solution.py:57
  681.6 56.0 %collective-permute-start.48 = (f32[2,2,128]{2,1,0:T(2,128)S(1)}, f32[2,2,128]{2,1,0:T(2,128)S(1)}, u32[]{:S(2)}, u32[]{:S(2)}) collective-permute-start(f32[2,2,128]{2,1,0:T(2,128)S(1)} %slice_bitcast_fusion.17), channel_id=1, source_target_pairs={{0,4},{2,6},{4,0},{6,2},{8,12},{10,14},{12,8},{14,10},{16,20},{18,... | collective-permute-start | bytes 6152 | tf_op jit(solution)/shard_map/ppermute | solution.py:57
  686.7 73.4 %collective-permute-start.59 = (bf16[2,2,128,1024]{2,3,1,0:T(8,128)(2,1)}, bf16[2,2,128,1024]{2,3,1,0:T(8,128)(2,1)}, u32[]{:S(2)}, u32[]{:S(2)}) collective-permute-start(bf16[2,2,128,1024]{2,3,1,0:T(8,128)(2,1)} %copy.80), channel_id=1, source_target_pairs={{0,4},{2,6},{4,0},{6,2},{8,12},{10,14},{12,8},{14,10},{16,20},{18,... | collective-permute-start | bytes 3145736 | tf_op jit(solution)/shard_map/ppermute | solution.py:57
  745.7 59.2 %collective-permute-start.76 = (bf16[512,2048]{1,0:T(8,128)(2,1)}, bf16[512,2048]{1,0:T(8,128)(2,1)S(1)}, u32[]{:S(2)}, u32[]{:S(2)}) collective-permute-start(bf16[512,2048]{1,0:T(8,128)(2,1)} %slice.488), channel_id=1, source_target_pairs={{0,4},{2,6},{4,0},{6,2},{8,12},{10,14},{12,8},{14,10},{16,20},{18,... | collective-permute-start | bytes 6291464 | tf_op jit(solution)/shard_map/ppermute | solution.py:57
  766.1 55.9 %collective-permute-start.55 = (bf16[2,2,128,768]{3,2,0,1:T(8,128)(2,1)S(1)}, bf16[2,2,128,768]{3,2,0,1:T(8,128)(2,1)S(1)}, u32[]{:S(2)}, u32[]{:S(2)}) collective-permute-start(bf16[2,2,128,768]{3,2,0,1:T(8,128)(2,1)S(1)} %bitcast.418), channel_id=1, source_target_pairs={{0,8},{2,10},{4,12},{6,14},{8,0},{10,2},{12,4},{14,6},{16,24},{18,... | collective-permute-start | bytes 2359304 | tf_op jit(solution)/shard_map/ppermute | solution.py:57
  787.0 34.4 %collective-permute-start.52 = (bf16[2,2,128,768]{3,2,1,0:T(8,128)(2,1)S(1)}, bf16[2,2,128,768]{3,2,1,0:T(8,128)(2,1)S(1)}, u32[]{:S(2)}, u32[]{:S(2)}) collective-permute-start(bf16[2,2,128,768]{3,2,1,0:T(8,128)(2,1)S(1)} %bitcast.419), channel_id=1, source_target_pairs={{0,4},{2,6},{4,0},{6,2},{8,12},{10,14},{12,8},{14,10},{16,20},{18,... | collective-permute-start | bytes 2359304 | tf_op jit(solution)/shard_map/ppermute | solution.py:57
  787.6 37.2 %collective-permute-start.61 = (bf16[128,1024]{0,1:T(8,128)(2,1)S(1)}, bf16[128,1024]{0,1:T(8,128)(2,1)S(1)}, u32[]{:S(2)}, u32[]{:S(2)}) collective-permute-start(bf16[128,1024]{0,1:T(8,128)(2,1)S(1)} %dynamic-slice_bitcast_fusion), channel_id=1, source_target_pairs={{0,8},{2,10},{4,12},{6,14},{8,0},{10,2},{12,4},{14,6},{16,24},{18,... | collective-permute-start | bytes 786440 | tf_op jit(solution)/shard_map/ppermute | solution.py:57
  790.4 179.4 %collective-permute-start.69 = (bf16[256,2048]{1,0:T(8,128)(2,1)S(1)}, bf16[256,2048]{1,0:T(8,128)(2,1)S(1)}, u32[]{:S(2)}, u32[]{:S(2)}) collective-permute-start(bf16[256,2048]{1,0:T(8,128)(2,1)S(1)} %slice.480), channel_id=1, source_target_pairs={{0,16},{2,18},{4,20},{6,22},{8,24},{10,26},{12,28},{14,30},{16,0},... | collective-permute-start | bytes 3145736 | tf_op jit(solution)/shard_map/ppermute | solution.py:57
  804.9 166.4 %collective-permute-start.73 = (bf16[256,2048]{1,0:T(8,128)(2,1)}, bf16[256,2048]{1,0:T(8,128)(2,1)}, u32[]{:S(2)}, u32[]{:S(2)}) collective-permute-start(bf16[256,2048]{1,0:T(8,128)(2,1)} %slice.484), channel_id=1, source_target_pairs={{0,16},{2,18},{4,20},{6,22},{8,24},{10,26},{12,28},{14,30},{16,0},... | collective-permute-start | bytes 3145736 | tf_op jit(solution)/shard_map/ppermute | solution.py:57
  821.4 156.9 %collective-permute-start.77 = (bf16[256,2048]{1,0:T(8,128)(2,1)}, bf16[256,2048]{1,0:T(8,128)(2,1)}, u32[]{:S(2)}, u32[]{:S(2)}) collective-permute-start(bf16[256,2048]{1,0:T(8,128)(2,1)} %slice.490), channel_id=1, source_target_pairs={{0,16},{2,18},{4,20},{6,22},{8,24},{10,26},{12,28},{14,30},{16,0},... | collective-permute-start | bytes 3145736 | tf_op jit(solution)/shard_map/ppermute | solution.py:57
  822.0 133.0 %collective-permute-start.53 = (bf16[2,128,768]{2,1,0:T(8,128)(2,1)S(1)}, bf16[2,128,768]{2,1,0:T(8,128)(2,1)S(1)}, u32[]{:S(2)}, u32[]{:S(2)}) collective-permute-start(bf16[2,128,768]{2,1,0:T(8,128)(2,1)S(1)} %slice_bitcast_fusion.7), channel_id=1, source_target_pairs={{0,16},{2,18},{4,20},{6,22},{8,24},{10,26},{12,28},{14,30},{16,0},... | collective-permute-start | bytes 1179656 | tf_op jit(solution)/shard_map/ppermute | solution.py:57
  824.8 137.4 %collective-permute-start.56 = (bf16[2,128,768]{2,1,0:T(8,128)(2,1)S(1)}, bf16[2,128,768]{2,1,0:T(8,128)(2,1)S(1)}, u32[]{:S(2)}, u32[]{:S(2)}) collective-permute-start(bf16[2,128,768]{2,1,0:T(8,128)(2,1)S(1)} %slice_bitcast_fusion.5), channel_id=1, source_target_pairs={{0,16},{2,18},{4,20},{6,22},{8,24},{10,26},{12,28},{14,30},{16,0},... | collective-permute-start | bytes 1179656 | tf_op jit(solution)/shard_map/ppermute | solution.py:57
  (131 other events, 1887.8 us)
